TPU v7x, 512 devices: a whole 4x4x16 slice. The times are simulated.
512 devices in a mesh: space: 128 (over x, z, core), col: 4 (over y).
Axes of the slice: x: 4, y: 4, z: 16, core: 2. Of those that a mesh axis runs over, the one named last changes fastest.
Arguments:
- panel: float32 [128, 983040], P(None, ('space', 'col')), may hold values from -6 to 1008
- trailing: float32 [256, 983040], P('col', 'space'), may hold values from -6 to 6
Outputs:
- upper_factor: float32 [128, 128], replicated
- updated: float32 [256, 983040], P('col', 'space')
All inputs are finite; a program needn't handle non-finite values.
Results may differ from a plain program's by a relative error of at most 0.00007.
Values sent between devices are 32-bit elements; how exact they have to be, the bound alone decides.
A program may use at most 64 MiB of HBM per device.

v0:
```python
import math

import jax
import jax.numpy as jnp
from jax import lax
from jax.sharding import PartitionSpec as P

highest = lax.Precision.HIGHEST


def spread(array, axis, root):
    mine = lax.axis_index(axis) == root
    return lax.psum(jnp.where(mine, array, jnp.zeros_like(array)), axis)


def solve_lower(lower_factor, right_side):
    return jax.scipy.linalg.solve_triangular(lower_factor, right_side, lower=True)


def solve_kernel(top_block, coupling):
    width = top_block.shape[0]
    kernel_matrix = jnp.eye(width, dtype=jnp.float32) + top_block
    normal_matrix = jnp.dot(kernel_matrix.T, kernel_matrix, precision=highest)
    chol_factor = jnp.linalg.cholesky(normal_matrix)
    right_side = jnp.dot(kernel_matrix.T, coupling, precision=highest)
    return jax.scipy.linalg.cho_solve((chol_factor, True), right_side)


def per_device(panel, trailing):
    width = panel.shape[0]
    gathered = lax.all_gather(panel, "col", axis=1, tiled=True)
    rows_total = gathered.shape[1] * lax.axis_size("space")
    indicator = (lax.axis_index("space") == 0).astype(jnp.float32)
    gram_total = lax.psum(jnp.dot(gathered, gathered.T, precision=highest), "space")
    lower_factor = jnp.linalg.cholesky(gram_total)
    scaled = solve_lower(lower_factor, gathered)
    basis = scaled.at[:, :width].add(jnp.eye(width, dtype=jnp.float32) * indicator)
    top_rows = spread(scaled[:, :width], "space", 0)
    coupling = lax.psum(jnp.dot(basis, trailing.T, precision=highest), "space")
    weights = solve_kernel(top_rows.T, coupling)
    updated = trailing - jnp.dot(weights.T, basis, precision=highest)
    upper_factor = -lower_factor.T / math.sqrt(rows_total)
    return (upper_factor, updated)


def solution(mesh):
    return jax.shard_map(
        per_device,
        mesh=mesh,
        in_specs=(P(None, ("space", "col")), P("col", "space")),
        out_specs=(P(), P("col", "space")),
        check_vma=False,
    )
```

profile of v0, /device:TPU:1, one launch (start us, length us, event | category | flops | bytes accessed | tf_op | source)
XLA Modules:
  0.0 953.7 jit_solution(6672607156562390368)
XLA Ops:
  7.2 0.0 all-gather.2.cloned.1.call-start
  7.2 0.7 all-gather.2.cloned.1.call-update
  7.9 0.0 all-reduce.3.cloned.1.call-start
  7.9 61.2 %all-gather.2.cloned.1.call-done = f32[128,7680]{1,0:T(8,128)} async-done(((f32[128,1920]{1,0:T(8,128)}), f32[128,7680]{1,0:T(8,128)}) %all-gather.2.cloned.1.call-update) | async-done | bytes 3932176 | tf_op jit(solution)/shard_map/all_gather | solution.py:31
  69.2 7.2 fusion.14
  76.4 0.0 all-reduce.3.cloned.1.call-update
  76.4 0.0 all-reduce.5.cloned.1.call-start
  76.5 0.1 copy.7
  76.6 0.9 compare_reduce_fusion.2
  77.5 309.3 %all-reduce.3.cloned.1.call-done = f32[128,128]{0,1:T(8,128)} async-done(((f32[128,128]{0,1:T(8,128)}), f32[128,128]{0,1:T(8,128)}) %all-reduce.3.cloned.1.call-update) | async-done | bytes 65552 | tf_op jit(solution)/shard_map/psum | solution.py:34
  386.8 0.9 copy.5
  387.7 0.9 fusion.9
  388.6 11.7 %cholesky.44 = f32[128,128]{1,0:T(8,128)S(1)} custom-call(f32[128,128]{1,0:T(8,128)S(1)} %fusion.9), custom_call_target="Cholesky" | custom-call | tf_op jit(solution)/shard_map/jit(cholesky)/cholesky | solution.py:35
  400.3 0.6 compare_reduce_fusion.1
  401.0 0.7 fusion.11
  401.7 9.8 %custom-call.13 = f32[1,128,128]{1,2,0:T(8,128)S(1)} custom-call(f32[1,128,128]{2,1,0:T(8,128)S(1)} %get-tuple-element.19), custom_call_target="InvertDiagBlocksLowerTriangular" | custom-call | tf_op jit(solution)/shard_map/jit(_solve_triangular)/triangular_solve | solution.py:17
  411.5 0.0 copy-start
  411.5 7.7 fusion.7
  419.1 2.1 select_bitcast_fusion
  421.3 0.0 all-reduce.5.cloned.1.call-update
  421.3 0.0 copy-done
  421.3 5.5 fusion.15
  426.9 0.7 copy.8
  427.6 488.3 %psum.23 = f32[128,64]{1,0:T(8,128)S(1)} all-reduce(f32[128,64]{1,0:T(8,128)S(1)} %fusion.15), channel_id=1, replica_groups=mesh['space'=128,'col'=4] {'space'}, use_global_device_ids=true, to_apply=%region_5.7 | all-reduce | flops 8192 | bytes 65536 | tf_op jit(solution)/shard_map/psum | solution.py:39
  915.9 0.0 all-reduce.5.cloned.1.call-done
  915.9 1.2 fusion.13
  917.1 0.1 copy.6
  917.2 11.7 %cholesky.55 = f32[128,128]{1,0:T(8,128)S(1)} custom-call(f32[128,128]{1,0:T(8,128)S(1)} %fusion.6), custom_call_target="Cholesky" | custom-call | tf_op jit(solution)/shard_map/jit(cholesky)/cholesky | solution.py:24
  929.0 0.6 compare_reduce_fusion
  929.6 0.7 fusion
  930.3 9.8 %custom-call.14 = f32[1,128,128]{1,2,0:T(8,128)S(1)} custom-call(f32[1,128,128]{2,1,0:T(8,128)S(1)} %fusion), custom_call_target="InvertDiagBlocksLowerTriangular" | custom-call | tf_op jit(solution)/shard_map/jit(_cho_solve)/triangular_solve | solution.py:26
  940.1 1.0 fusion.12
  941.2 0.3 fusion.4
  941.4 0.2 fusion.2
  941.7 5.5 convolution_subtract_fusion
  (4 shorter events, 0.1 us)
Async XLA Ops:
  7.2 62.0 %all-gather.2.cloned.1.call-start = ((), (), s32[]{:S(2)}) async-start(), calls=%async_computation | async-start | bytes 4915200 | tf_op jit(solution)/shard_map/all_gather | solution.py:31
  7.9 378.9 %all-reduce.3.cloned.1.call-start = ((), (), s32[]{:S(2)}) async-start(), calls=%async_computation.1 | async-start | bytes 131072 | tf_op jit(solution)/shard_map/psum | solution.py:34
  76.4 839.5 %all-reduce.5.cloned.1.call-start = ((), (), s32[]{:S(2)}) async-start(), calls=%async_computation.2 | async-start | bytes 131072 | tf_op jit(solution)/shard_map/psum | solution.py:13
  411.5 9.8 %copy-start = (f32[64,7680]{1,0:T(8,128)S(1)}, f32[64,7680]{1,0:T(8,128)}, u32[]{:S(2)}) copy-start(f32[64,7680]{1,0:T(8,128)} %param.6) | copy-start | bytes 5898244
Sparse Core Ops, SparseCore 0:
  10.1 59.0 all-gather.1
  76.6 310.1 all-reduce.2
  421.4 302.3 all-reduce.4
where the time goes:
time: 958 us; the launch traced here: 954 us
  blocking collectives  488 us (51%)
  waiting for transfers between devices  371 us (39%)
  other arithmetic  49.6 us (5%)
  matrix products  28.7 us (3%)
  between operations  13.9 us (1%)
    psum x1, blocking collectives, per_device(): coupling = lax.psum(jnp.dot(basis, trailing.T, precision=highest), 'space')  488 us
    psum x1, waiting for transfers between devices, per_device(): lax.psum(jnp.dot(gathered, gathered.T, precision=highest), 'space')  309 us
    all_gather x1, waiting for transfers between devices, per_device(): gathered = lax.all_gather(panel, 'col', axis=1, tiled=True)  61.2 us
  transfers between devices with their start and end apart: 3, of which 2 were waited for; matrix products, arithmetic and copies ran while one was open for 1% of the time, Pallas kernels for 0%

commit v1 on v0

v1 whole, which is shorter than its diff:
```python
import functools
import math

import jax
import jax.numpy as jnp
from jax import lax
from jax.experimental import pallas as pl
from jax.experimental.pallas import tpu as pltpu
from jax.sharding import PartitionSpec as P

F32 = jnp.float32
BF16 = jnp.bfloat16
HIGHEST = lax.Precision.HIGHEST
MESH = pl.DeviceIdType.MESH
NX, NZ, NCORE, NY = 4, 16, 2, 4
PLANE = NX * NY * NCORE
PAIRS = NX * NCORE
BLK = 8


def split2(x):
    high = x.astype(BF16)
    low = (x - high.astype(F32)).astype(BF16)
    return high, low


def split3(x):
    high = x.astype(BF16).astype(F32)
    rest = x - high
    mid = rest.astype(BF16).astype(F32)
    return high, mid, rest - mid


def stacks(a, b):
    ah, am, al = split3(a)
    bh, bm, bl = split3(b)
    left = jnp.concatenate([ah, ah, ah, am, am, al], axis=0).astype(BF16)
    right = jnp.concatenate([bh, bm, bl, bh, bm, bh], axis=0).astype(BF16)
    return left, right


def dot_tn(a, b):
    return lax.dot_general(a, b, (((0,), (0,)), ((), ())), preferred_element_type=F32)


def dot_nt(a, b):
    return lax.dot_general(a, b, (((1,), (1,)), ((), ())), preferred_element_type=F32)


def recip(x):
    y = pl.reciprocal(x, approx=True)
    return y * (2.0 - x * y)


def lane_splat(x, lane):
    return jnp.take_along_axis(x, jnp.full(x.shape, lane, jnp.int32), axis=1)


def merge(rows, row8):
    out = rows[0]
    for i in range(1, len(rows)):
        out = jnp.where(row8 == i, rows[i], out)
    return out


def block_rows(ref, base):
    width = ref.shape[1]
    return [jnp.broadcast_to(ref[pl.ds(base + i, 1), :], (BLK, width)) for i in range(BLK)]


def chol_step(k, work, upper):
    width = work.shape[1]
    row8 = lax.broadcasted_iota(jnp.int32, (BLK, width), 0)
    lane8 = lax.broadcasted_iota(jnp.int32, (BLK, width), 1)
    base = pl.multiple_of(k * BLK, BLK)
    rows = block_rows(work, base)
    s = {(i, j): lane_splat(rows[i], base + j) for i in range(BLK) for j in range(i, BLK)}
    for j in range(BLK):
        inv = recip(s[j, j])
        for i in range(j + 1, BLK):
            factor = s[j, i] * inv
            for l in range(i, BLK):
                s[i, l] = s[i, l] - factor * s[j, l]
            rows[i] = rows[i] - factor * rows[j]
    pivots = merge([s[j, j] for j in range(BLK)], row8)
    block = merge(rows, row8) * lax.rsqrt(pivots)
    block = jnp.where(lane8 >= row8 + base, block, 0.0)
    upper[pl.ds(base, BLK), :] = block
    left, right = stacks(block, block)
    work[...] -= dot_tn(left, right)


def inverse_step(k, mat, mat_t):
    width = mat.shape[1]
    row8 = lax.broadcasted_iota(jnp.int32, (BLK, width), 0)
    lane8 = lax.broadcasted_iota(jnp.int32, (BLK, width), 1)
    base = pl.multiple_of(k * BLK, BLK)
    rows = block_rows(mat, base)
    cols = mat_t[pl.ds(base, BLK), :]
    s = {(i, j): lane_splat(rows[i], base + j) for i in range(BLK) for j in range(BLK)}
    for j in range(BLK):
        inv = recip(s[j, j])
        at = lane8 == base + j
        scaled = jnp.where(at, 1.0, rows[j]) * inv
        for l in range(j + 1, BLK):
            s[j, l] = s[j, l] * inv
        for i in range(BLK):
            if i == j:
                continue
            for l in range(j + 1, BLK):
                s[i, l] = s[i, l] - s[i, j] * s[j, l]
            rows[i] = jnp.where(at, 0.0, rows[i]) - s[i, j] * scaled
        rows[j] = scaled
    block = merge(rows, row8)
    inside = (lane8 >= base) & (lane8 < base + BLK)
    cols = jnp.where(inside, jnp.where(lane8 == row8 + base, -1.0, 0.0), cols)
    left, right = stacks(cols, block)
    row_id = lax.broadcasted_iota(jnp.int32, (width, width), 0)
    lane_id = lax.broadcasted_iota(jnp.int32, (width, width), 1)
    row_out = (row_id < base) | (row_id >= base + BLK)
    lane_out = (lane_id < base) | (lane_id >= base + BLK)
    keep = row_out & lane_out
    mat[...] = jnp.where(keep, mat[...], 0.0) - dot_tn(left, right)
    mat_t[...] = jnp.where(keep, mat_t[...], 0.0) - dot_tn(right, left)


def main_kernel(p_hbm, t_hbm, gat_out, upper, zt,
                gat, tv, g_loc, zr, pr, gf, p1t, p1f, m_loc, mr, mz, zsum, work, work_t,
                gp_send, gp_recv, loc, out_sem, st_send, st_recv):
    width, part = p_hbm.shape
    half = width // 2
    space = lax.axis_index("space")
    y = lax.axis_index("col")
    core = space % NCORE
    z = (space // NCORE) % NZ
    x = space // (NCORE * NZ)
    pair = x * NCORE + core
    plane = pair * NY + y
    right, left, far = (y + 1) % NY, (y + NY - 1) % NY, (y + 2) % NY

    def at_z(zz):
        return (x * (NZ * NCORE) + zz * NCORE + core, y)

    def at_plane(q):
        px = q // (NCORE * NY)
        pc = (q // NY) % NCORE
        return (px * (NZ * NCORE) + z * NCORE + pc, q % NY)

    def at_pair(q):
        return ((q // NCORE) * (NZ * NCORE) + z * NCORE + q % NCORE, y)

    def loop(low, high, body):
        lax.fori_loop(low, high, lambda i, c: (body(i), c)[1], 0)

    def send(src, dst, stage, device):
        pltpu.make_async_remote_copy(
            src_ref=src, dst_ref=dst, send_sem=st_send.at[stage], recv_sem=st_recv.at[stage],
            device_id=device, device_id_type=MESH).start()

    def settle(ref, sem):
        pltpu.make_async_copy(ref, ref, sem).wait()

    def rows8(i):
        return pl.ds(pl.multiple_of(i * BLK, BLK), BLK)

    barrier = pltpu.get_barrier_semaphore()

    def greet(device):
        pl.semaphore_signal(barrier, inc=1, device_id=device, device_id_type=MESH)

    own = pltpu.make_async_copy(p_hbm, gat.at[y], loc.at[0])
    own.start()
    loads = [pltpu.make_async_copy(t_hbm.at[:, pl.ds(c * part, part)], tv.at[c], loc.at[1 + c])
             for c in range(NY)]
    for load in loads:
        load.start()
    loop(1, PLANE, lambda d: greet(at_plane((plane + d) % PLANE)))
    loop(1, NZ, lambda d: greet(at_z((z + d) % NZ)))
    pl.semaphore_wait(barrier, PLANE + NZ - 2)

    first, second = pl.ds(0, half), pl.ds(half, half)

    def gather_copy(src, dst, index, target):
        return pltpu.make_async_remote_copy(
            src_ref=src, dst_ref=dst, send_sem=gp_send.at[index], recv_sem=gp_recv.at[index],
            device_id=(space, target), device_id_type=MESH)

    ra = gather_copy(p_hbm.at[first], gat.at[y, first], 0, right)
    lb = gather_copy(p_hbm.at[second], gat.at[y, second], 1, left)
    rb = gather_copy(p_hbm.at[second], gat.at[y, second], 2, right)
    la = gather_copy(p_hbm.at[first], gat.at[y, first], 3, left)
    for copy in (ra, lb, rb, la):
        copy.start()
    own.wait()
    high, low = split2(gat[y])
    both = dot_nt(high, jnp.concatenate([high, low], axis=0))
    cross = both[:, width:]
    g_loc[...] = both[:, :width] + cross + cross.T

    loop(1, NZ, lambda d: send(g_loc.at[rows8((z + d) % NZ)], zr.at[d - 1], 0, at_z((z + d) % NZ)))

    @pl.when((plane == 0) & (z == 0))
    def _():
        loop(1, NZ, lambda d: send(gat.at[0, rows8(d), pl.ds(0, width)], p1t, 3, at_z(d)))
        p1t[...] = gat[0, 0:BLK, 0:width]

    settle(zr, st_recv.at[0])
    total = g_loc[rows8(z), :]
    for d in range(NZ - 1):
        total = total + zr[d]
    pr[plane] = total
    loop(1, PLANE, lambda d: send(pr.at[plane], pr.at[plane], 1, at_plane((plane + d) % PLANE)))

    @pl.when((plane == 0) & (z > 0))
    def _():
        settle(p1t, st_recv.at[3])

    @pl.when(plane == 0)
    def _():
        loop(1, PLANE, lambda d: send(p1t, p1t, 4, at_plane(d)))

    settle(pr.at[pl.ds(0, PLANE - 1)], st_recv.at[1])
    total = pr[0]
    for q in range(1, PLANE):
        total = total + pr[q]
    gf[rows8(z), :] = total
    loop(1, NZ, lambda d: send(gf.at[rows8(z)], gf.at[rows8(z)], 2, at_z((z + d) % NZ)))

    @pl.when(plane > 0)
    def _():
        settle(p1t, st_recv.at[4])

    p1f[rows8(z), :] = p1t[...]
    loop(1, NZ, lambda d: send(p1f.at[rows8(z)], p1f.at[rows8(z)], 5, at_z((z + d) % NZ)))

    settle(gf.at[pl.ds(0, (NZ - 1) * BLK)], st_recv.at[2])
    work[...] = gf[...]
    ra.wait_recv()
    fa = gather_copy(gat.at[left, first], gat.at[left, first], 4, right)
    fa.start()
    lb.wait_recv()
    fb = gather_copy(gat.at[right, second], gat.at[right, second], 5, left)
    fb.start()
    loop(0, width // BLK, lambda k: chol_step(k, work, upper))

    settle(p1f.at[pl.ds(0, (NZ - 1) * BLK)], st_recv.at[5])
    work[...] = gf[...] + jnp.dot(p1f[...], upper[...], precision=HIGHEST, preferred_element_type=F32)
    work_t[...] = work[...].T
    loop(0, width // BLK, lambda k: inverse_step(k, work, work_t))

    for load in loads:
        load.wait()

    def products(c):
        ph, pl_ = split2(gat[c])
        th, tl = split2(tv[c])
        four = dot_nt(jnp.concatenate([th, tl], axis=0), jnp.concatenate([ph, pl_], axis=0))
        rows = th.shape[0]
        return (four[:rows, :width] + four[rows:, :width]) + (four[:rows, width:] + four[rows:, width:])

    def put_out(c, index):
        copy = pltpu.make_async_copy(gat.at[c], gat_out.at[c], out_sem.at[index])
        copy.start()
        return copy

    m_loc[...] = products(y)
    outs = [put_out(y, 0)]

    @pl.when(space == 0)
    def _():
        m_loc[...] += jnp.dot(tv[0, :, 0:width], upper[...], precision=HIGHEST,
                              preferred_element_type=F32)

    rb.wait_recv()
    m_loc[...] += products(left)
    outs.append(put_out(left, 1))
    la.wait_recv()
    m_loc[...] += products(right)
    outs.append(put_out(right, 2))
    fa.wait_recv()
    fb.wait_recv()
    m_loc[...] += products(far)
    outs.append(put_out(far, 3))

    loop(1, PAIRS, lambda d: send(m_loc.at[rows8((pair + d) % PAIRS)], mr.at[d - 1], 6,
                                  at_pair((pair + d) % PAIRS)))
    settle(mr, st_recv.at[6])
    total = m_loc[rows8(pair), :]
    for d in range(PAIRS - 1):
        total = total + mr[d]
    mz[z] = total
    loop(1, NZ, lambda d: send(mz.at[z], mz.at[z], 7, at_z((z + d) % NZ)))
    settle(mz.at[pl.ds(0, NZ - 1)], st_recv.at[7])
    total = mz[0]
    for q in range(1, NZ):
        total = total + mz[q]
    zsum[rows8(pair), :] = jnp.dot(total, work[...], precision=HIGHEST, preferred_element_type=F32)
    loop(1, PAIRS, lambda d: send(zsum.at[rows8(pair)], zsum.at[rows8(pair)], 8,
                                  at_pair((pair + d) % PAIRS)))
    settle(zsum.at[pl.ds(0, (PAIRS - 1) * BLK)], st_recv.at[8])
    zt[...] = zsum[...]

    for copy in (ra, lb, rb, la, fa, fb):
        copy.wait_send()
    for copy in outs:
        copy.wait()
    settle(zr, st_send.at[0])
    settle(pr.at[pl.ds(0, PLANE - 1)], st_send.at[1])
    settle(gf.at[pl.ds(0, (NZ - 1) * BLK)], st_send.at[2])

    @pl.when((plane == 0) & (z == 0))
    def _():
        settle(gf.at[pl.ds(0, (NZ - 1) * BLK)], st_send.at[3])

    @pl.when(plane == 0)
    def _():
        settle(pr.at[pl.ds(0, PLANE - 1)], st_send.at[4])

    settle(gf.at[pl.ds(0, (NZ - 1) * BLK)], st_send.at[5])
    settle(mr, st_send.at[6])
    settle(mz.at[pl.ds(0, NZ - 1)], st_send.at[7])
    settle(mr, st_send.at[8])


def update_kernel(scale, p_ref, t_ref, zt_ref, upper_ref, up_ref, out_ref):
    zt = zt_ref[...]
    rows = zt.shape[0]
    width = zt.shape[1]
    zh, zl = split2(zt)
    ph, pl_ = split2(p_ref[0])
    double = jnp.dot(jnp.concatenate([zh, zl], axis=0), ph, preferred_element_type=F32)
    cross = jnp.dot(zh, pl_, preferred_element_type=F32)
    out_ref[...] = t_ref[...] - (double[:rows] + (double[rows:] + cross))

    @pl.when(pl.program_id(0) == 0)
    def _():
        up_ref[...] = upper_ref[...] * scale

    @pl.when((pl.program_id(0) == 0) & (lax.axis_index("space") == 0))
    def _():
        out_ref[:, 0:width] -= lax.dot_general(
            zt, upper_ref[...], (((1,), (1,)), ((), ())), precision=HIGHEST,
            preferred_element_type=F32)


def per_device(panel, trailing):
    width, part = panel.shape
    rows, block = trailing.shape
    rows_total = block * lax.axis_size("space")
    vmem = pl.BlockSpec(memory_space=pltpu.VMEM)
    hbm = pl.BlockSpec(memory_space=pl.ANY)

    def buf(*shape):
        return pltpu.VMEM(shape, F32)

    gat, upper, zt = pl.pallas_call(
        main_kernel,
        out_shape=(
            jax.ShapeDtypeStruct((NY, width, part), F32),
            jax.ShapeDtypeStruct((width, width), F32),
            jax.ShapeDtypeStruct((rows, width), F32),
        ),
        in_specs=[hbm, hbm],
        out_specs=(hbm, vmem, vmem),
        scratch_shapes=[
            buf(NY, width, part),
            buf(NY, rows, part),
            buf(width, width),
            buf(NZ - 1, BLK, width),
            buf(PLANE, BLK, width),
            buf(width, width),
            buf(BLK, width),
            buf(width, width),
            buf(rows, width),
            buf(PAIRS - 1, BLK, width),
            buf(NZ, BLK, width),
            buf(rows, width),
            buf(width, width),
            buf(width, width),
            pltpu.SemaphoreType.DMA((6,)),
            pltpu.SemaphoreType.DMA((6,)),
            pltpu.SemaphoreType.DMA((1 + NY,)),
            pltpu.SemaphoreType.DMA((NY,)),
            pltpu.SemaphoreType.DMA((9,)),
            pltpu.SemaphoreType.DMA((9,)),
        ],
        compiler_params=pltpu.CompilerParams(
            collective_id=0, has_side_effects=True, vmem_limit_bytes=40 * 2**20),
        name="reduce_factor",
    )(panel, trailing)

    upper_factor, updated = pl.pallas_call(
        functools.partial(update_kernel, -1.0 / math.sqrt(rows_total)),
        grid=(NY,),
        out_shape=(
            jax.ShapeDtypeStruct((width, width), F32),
            jax.ShapeDtypeStruct((rows, block), F32),
        ),
        in_specs=[
            pl.BlockSpec((1, width, part), lambda i: (i, 0, 0)),
            pl.BlockSpec((rows, part), lambda i: (0, i)),
            pl.BlockSpec((rows, width), lambda i: (0, 0)),
            pl.BlockSpec((width, width), lambda i: (0, 0)),
        ],
        out_specs=(
            pl.BlockSpec((width, width), lambda i: (0, 0)),
            pl.BlockSpec((rows, part), lambda i: (0, i)),
        ),
        compiler_params=pltpu.CompilerParams(vmem_limit_bytes=40 * 2**20),
        name="apply_update",
    )(gat, trailing, zt, upper)
    return (upper_factor, updated)


def solution(mesh):
    return jax.shard_map(
        per_device,
        mesh=mesh,
        in_specs=(P(None, ("space", "col")), P("col", "space")),
        out_specs=(P(), P("col", "space")),
        check_vma=False,
    )
```

time: 958 us -> 92.7 us (0.10)
  blocking collectives: 488 us -> 0 us
  waiting for transfers between devices: 371 us -> 0 us
  Pallas kernels: 0 us -> 89.1 us
  other arithmetic: 49.6 us -> 0 us
  matrix products: 28.7 us -> 0 us
  between operations: 13.9 us -> 0.66 us
    psum x1 -> x0, blocking collectives: 488 us -> none  [per_device(): coupling = lax.psum(jnp.dot(basis, trailing.T, precision=highest), 'space')]
    psum x2 -> x0, waiting for transfers between devices: 309 us -> none  [the longest x1 309 us: per_device(): lax.psum(jnp.dot(gathered, gathered.T, precision=highest), 'space')]
    pallas_call x0 -> x2, Pallas kernels: none -> 89.1 us  [the longest x1 86.3 us: per_device(): pl.pallas_call(main_kernel, out_shape=(jax.ShapeDtypeStruct((NY, width, p...]
    all_gather x1 -> x0, waiting for transfers between devices: 61.2 us -> none  [per_device(): gathered = lax.all_gather(panel, 'col', axis=1, tiled=True)]
    another operation x11 -> x0, other arithmetic: 46.6 us -> none  [the longest x3 12.4 us: per_device(): lower_factor = jnp.linalg.cholesky(gram_total)]
    dot_general x5 -> x0, matrix products: 20.5 us -> none  [the longest x1 7.23 us: per_device(): jnp.dot(gathered, gathered.T, precision=highest)]
  transfers between devices with their start and end apart: 3 -> 0, of which waited for: 2 -> 0; matrix products, arithmetic and copies ran while one was open for 1% -> 0% of each run, Pallas kernels for 0% -> 0%
where the time goes in v1:
time: 92.7 us; the launch traced here: 92.5 us
  Pallas kernels  89.1 us (96%)
  local copies, waits for them, and re-layouts  2.74 us (3%)
    pallas_call x1, Pallas kernels, per_device(): pl.pallas_call(main_kernel, out_shape=(jax.ShapeDtypeStruct((NY, width, p...  86.3 us
    pallas_call x1, Pallas kernels, per_device(): pl.pallas_call(functools.partial(update_kernel, -1.0 / math.sqrt(rows_tot...  2.84 us
    unnamed x6, local copies, waits for them, and re-layouts  2.74 us

profile of v1, /device:TPU:1, one launch (start us, length us, event | category | flops | bytes accessed | tf_op | source)
XLA Modules:
  0.0 92.5 jit_solution(13923744765937615172)
XLA Ops:
  0.6 0.0 copy-start
  0.6 1.5 %copy-done = f32[64,7680]{1,0:T(8,128)S(1)} copy-done((f32[64,7680]{1,0:T(8,128)S(1)}, f32[64,7680]{1,0:T(8,128)}, u32[]{:S(2)}) %copy-start) | copy-done | bytes 1966104
  2.2 0.0 copy-start.2
  2.2 1.2 %copy-done.2 = f32[128,1920]{1,0:T(8,128)S(1)} copy-done((f32[128,1920]{1,0:T(8,128)S(1)}, f32[128,1920]{1,0:T(8,128)}, u32[]{:S(2)}) %copy-start.2) | copy-done | bytes 983064
  3.4 0.0 copy-start.1
  3.4 86.3 %reduce_factor.1 = (f32[4,128,1920]{2,1,0:T(8,128)S(1)}, f32[128,128]{1,0:T(8,128)S(1)}, f32[64,128]{1,0:T(8,128)S(1)}) custom-call(f32[128,1920]{1,0:T(8,128)S(1)} %copy-done.2, f32[64,7680]{1,0:T(8,128)S(1)} %copy-done), custom_call_target="tpu_custom_call" | custom-call | tf_op jit(solution)/shard_map/reduce_factor/pallas_call | solution.py:356
  89.7 0.0 copy-done.1
  89.7 2.8 %apply_update.1 = (f32[128,128]{1,0:T(8,128)}, f32[64,7680]{1,0:T(8,128)}) custom-call(f32[4,128,1920]{2,1,0:T(8,128)S(1)} %get-tuple-element.5.p_ref, f32[64,7680]{1,0:T(8,128)S(1)} %copy-done.1, f32[64,128]{1,0:T(8,128)S(1)} %get-tuple-element.6.zt_ref, f32[128,128]{1,0:T(8,128)S(1)} %get-tuple-element.7.upper_ref), custom_call_target="tpu_custom_call" | custom-call | tf_op jit(solution)/shard_map/apply_update/pallas_call | solution.py:392
Async XLA Ops:
  0.6 1.5 %copy-start = (f32[64,7680]{1,0:T(8,128)S(1)}, f32[64,7680]{1,0:T(8,128)}, u32[]{:S(2)}) copy-start(f32[64,7680]{1,0:T(8,128)} %t_ref.1) | copy-start | bytes 5898244
  2.2 1.2 %copy-start.2 = (f32[128,1920]{1,0:T(8,128)S(1)}, f32[128,1920]{1,0:T(8,128)}, u32[]{:S(2)}) copy-start(f32[128,1920]{1,0:T(8,128)} %p_hbm.1) | copy-start | bytes 2949124
  3.4 86.3 %copy-start.1 = (f32[64,7680]{1,0:T(8,128)S(1)}, f32[64,7680]{1,0:T(8,128)}, u32[]{:S(2)}) copy-start(f32[64,7680]{1,0:T(8,128)} %t_ref.1) | copy-start | bytes 5898244

commit v2 on v1

--- a/solution.py
+++ b/solution.py
@@ -16,6 +16,7 @@
 PLANE = NX * NY * NCORE
 PAIRS = NX * NCORE
 BLK = 8
+PIECE = 16
 
 
 def split2(x):
@@ -125,7 +126,7 @@
 
 
 def main_kernel(p_hbm, t_hbm, gat_out, upper, zt,
-                gat, tv, g_loc, zr, pr, gf, p1t, p1f, m_loc, mr, mz, zsum, work, work_t,
+                gat, tv, g_loc, pr, gz, gf, p1s, p1f, m_loc, mr, mz, zsum, work, work_t,
                 gp_send, gp_recv, loc, out_sem, st_send, st_recv):
     width, part = p_hbm.shape
     half = width // 2
@@ -137,6 +138,7 @@
     pair = x * NCORE + core
     plane = pair * NY + y
     right, left, far = (y + 1) % NY, (y + NY - 1) % NY, (y + 2) % NY
+    root = (space == 0) & (y == 0)
 
     def at_z(zz):
         return (x * (NZ * NCORE) + zz * NCORE + core, y)
@@ -160,8 +162,8 @@
     def settle(ref, sem):
         pltpu.make_async_copy(ref, ref, sem).wait()
 
-    def rows8(i):
-        return pl.ds(pl.multiple_of(i * BLK, BLK), BLK)
+    def rows_of(i, size):
+        return pl.ds(pl.multiple_of(i * size, size), size)
 
     barrier = pltpu.get_barrier_semaphore()
 
@@ -170,13 +172,30 @@
 
     own = pltpu.make_async_copy(p_hbm, gat.at[y], loc.at[0])
     own.start()
+    loop(1, NZ, lambda d: greet(at_z((z + d) % NZ)))
+    loop(1, PLANE, lambda d: greet(at_plane((plane + d) % PLANE)))
+    own.wait()
     loads = [pltpu.make_async_copy(t_hbm.at[:, pl.ds(c * part, part)], tv.at[c], loc.at[1 + c])
              for c in range(NY)]
     for load in loads:
         load.start()
-    loop(1, PLANE, lambda d: greet(at_plane((plane + d) % PLANE)))
-    loop(1, NZ, lambda d: greet(at_z((z + d) % NZ)))
+    high, low = split2(gat[y])
+    both = dot_nt(high, jnp.concatenate([high, low], axis=0))
+    cross = both[:, width:]
+    g_loc[...] = both[:, :width] + cross + cross.T
     pl.semaphore_wait(barrier, PLANE + NZ - 2)
+
+    def scatter(d):
+        q = (plane + d) % PLANE
+        send(g_loc.at[rows_of(q // NY, PIECE)], pr.at[plane], 0, at_plane(q))
+
+    loop(1, PLANE, scatter)
+
+    @pl.when(root)
+    def _():
+        loop(1, PLANE, lambda q: send(gat.at[0, rows_of(q // NY, PIECE), pl.ds(0, width)], p1s, 3,
+                                      at_plane(q)))
+        p1s[...] = gat[0, 0:PIECE, 0:width]
 
     first, second = pl.ds(0, half), pl.ds(half, half)
 
@@ -191,80 +210,71 @@
     la = gather_copy(p_hbm.at[first], gat.at[y, first], 3, left)
     for copy in (ra, lb, rb, la):
         copy.start()
-    own.wait()
-    high, low = split2(gat[y])
-    both = dot_nt(high, jnp.concatenate([high, low], axis=0))
-    cross = both[:, width:]
-    g_loc[...] = both[:, :width] + cross + cross.T
-
-    loop(1, NZ, lambda d: send(g_loc.at[rows8((z + d) % NZ)], zr.at[d - 1], 0, at_z((z + d) % NZ)))
-
-    @pl.when((plane == 0) & (z == 0))
-    def _():
-        loop(1, NZ, lambda d: send(gat.at[0, rows8(d), pl.ds(0, width)], p1t, 3, at_z(d)))
-        p1t[...] = gat[0, 0:BLK, 0:width]
-
-    settle(zr, st_recv.at[0])
-    total = g_loc[rows8(z), :]
-    for d in range(NZ - 1):
-        total = total + zr[d]
-    pr[plane] = total
-    loop(1, PLANE, lambda d: send(pr.at[plane], pr.at[plane], 1, at_plane((plane + d) % PLANE)))
-
-    @pl.when((plane == 0) & (z > 0))
-    def _():
-        settle(p1t, st_recv.at[3])
-
-    @pl.when(plane == 0)
-    def _():
-        loop(1, PLANE, lambda d: send(p1t, p1t, 4, at_plane(d)))
-
-    settle(pr.at[pl.ds(0, PLANE - 1)], st_recv.at[1])
+
+    pr[plane] = g_loc[rows_of(pair, PIECE), :]
+    settle(pr.at[pl.ds(0, PLANE - 1)], st_recv.at[0])
     total = pr[0]
     for q in range(1, PLANE):
         total = total + pr[q]
-    gf[rows8(z), :] = total
-    loop(1, NZ, lambda d: send(gf.at[rows8(z)], gf.at[rows8(z)], 2, at_z((z + d) % NZ)))
-
-    @pl.when(plane > 0)
-    def _():
-        settle(p1t, st_recv.at[4])
-
-    p1f[rows8(z), :] = p1t[...]
-    loop(1, NZ, lambda d: send(p1f.at[rows8(z)], p1f.at[rows8(z)], 5, at_z((z + d) % NZ)))
-
-    settle(gf.at[pl.ds(0, (NZ - 1) * BLK)], st_recv.at[2])
-    work[...] = gf[...]
+    gz[z] = total
+    loop(1, NZ, lambda d: send(gz.at[z], gz.at[z], 1, at_z((z + d) % NZ)))
+
+    @pl.when((z == 0) & (plane > 0))
+    def _():
+        settle(p1s, st_recv.at[3])
+
+    @pl.when(z == 0)
+    def _():
+        loop(1, NZ, lambda d: send(p1s, p1s, 4, at_z(d)))
+
+    for load in loads:
+        load.wait()
+
+    def products(c):
+        ph, pl_ = split2(gat[c])
+        th, tl = split2(tv[c])
+        four = dot_nt(jnp.concatenate([th, tl], axis=0), jnp.concatenate([ph, pl_], axis=0))
+        rows = th.shape[0]
+        return (four[:rows, :width] + four[rows:, :width]) + (four[:rows, width:] + four[rows:, width:])
+
+    def put_out(c, index):
+        copy = pltpu.make_async_copy(gat.at[c], gat_out.at[c], out_sem.at[index])
+        copy.start()
+        return copy
+
+    m_loc[...] = products(y)
+    outs = [put_out(y, 0)]
+
+    settle(gz.at[pl.ds(0, NZ - 1)], st_recv.at[1])
+    total = gz[0]
+    for q in range(1, NZ):
+        total = total + gz[q]
+    mine = rows_of(pair, PIECE)
+    gf[mine, :] = total
+    loop(1, PAIRS, lambda d: send(gf.at[mine], gf.at[mine], 2, at_pair((pair + d) % PAIRS)))
+
+    @pl.when(z > 0)
+    def _():
+        settle(p1s, st_recv.at[4])
+
+    p1f[mine, :] = p1s[...]
+    loop(1, PAIRS, lambda d: send(p1f.at[mine], p1f.at[mine], 5, at_pair((pair + d) % PAIRS)))
+
     ra.wait_recv()
     fa = gather_copy(gat.at[left, first], gat.at[left, first], 4, right)
     fa.start()
     lb.wait_recv()
     fb = gather_copy(gat.at[right, second], gat.at[right, second], 5, left)
     fb.start()
+
+    others = pl.ds(0, (PAIRS - 1) * PIECE)
+    settle(gf.at[others], st_recv.at[2])
+    work[...] = gf[...]
     loop(0, width // BLK, lambda k: chol_step(k, work, upper))
-
-    settle(p1f.at[pl.ds(0, (NZ - 1) * BLK)], st_recv.at[5])
+    settle(p1f.at[others], st_recv.at[5])
     work[...] = gf[...] + jnp.dot(p1f[...], upper[...], precision=HIGHEST, preferred_element_type=F32)
     work_t[...] = work[...].T
     loop(0, width // BLK, lambda k: inverse_step(k, work, work_t))
-
-    for load in loads:
-        load.wait()
-
-    def products(c):
-        ph, pl_ = split2(gat[c])
-        th, tl = split2(tv[c])
-        four = dot_nt(jnp.concatenate([th, tl], axis=0), jnp.concatenate([ph, pl_], axis=0))
-        rows = th.shape[0]
-        return (four[:rows, :width] + four[rows:, :width]) + (four[:rows, width:] + four[rows:, width:])
-
-    def put_out(c, index):
-        copy = pltpu.make_async_copy(gat.at[c], gat_out.at[c], out_sem.at[index])
-        copy.start()
-        return copy
-
-    m_loc[...] = products(y)
-    outs = [put_out(y, 0)]
 
     @pl.when(space == 0)
     def _():
@@ -282,10 +292,11 @@
     m_loc[...] += products(far)
     outs.append(put_out(far, 3))
 
-    loop(1, PAIRS, lambda d: send(m_loc.at[rows8((pair + d) % PAIRS)], mr.at[d - 1], 6,
+    loop(1, PAIRS, lambda d: send(m_loc.at[rows_of((pair + d) % PAIRS, BLK)], mr.at[d - 1], 6,
                                   at_pair((pair + d) % PAIRS)))
     settle(mr, st_recv.at[6])
-    total = m_loc[rows8(pair), :]
+    tile = rows_of(pair, BLK)
+    total = m_loc[tile, :]
     for d in range(PAIRS - 1):
         total = total + mr[d]
     mz[z] = total
@@ -294,9 +305,8 @@
     total = mz[0]
     for q in range(1, NZ):
         total = total + mz[q]
-    zsum[rows8(pair), :] = jnp.dot(total, work[...], precision=HIGHEST, preferred_element_type=F32)
-    loop(1, PAIRS, lambda d: send(zsum.at[rows8(pair)], zsum.at[rows8(pair)], 8,
-                                  at_pair((pair + d) % PAIRS)))
+    zsum[tile, :] = jnp.dot(total, work[...], precision=HIGHEST, preferred_element_type=F32)
+    loop(1, PAIRS, lambda d: send(zsum.at[tile], zsum.at[tile], 8, at_pair((pair + d) % PAIRS)))
     settle(zsum.at[pl.ds(0, (PAIRS - 1) * BLK)], st_recv.at[8])
     zt[...] = zsum[...]
 
@@ -304,19 +314,19 @@
         copy.wait_send()
     for copy in outs:
         copy.wait()
-    settle(zr, st_send.at[0])
-    settle(pr.at[pl.ds(0, PLANE - 1)], st_send.at[1])
-    settle(gf.at[pl.ds(0, (NZ - 1) * BLK)], st_send.at[2])
-
-    @pl.when((plane == 0) & (z == 0))
-    def _():
-        settle(gf.at[pl.ds(0, (NZ - 1) * BLK)], st_send.at[3])
-
-    @pl.when(plane == 0)
-    def _():
-        settle(pr.at[pl.ds(0, PLANE - 1)], st_send.at[4])
-
-    settle(gf.at[pl.ds(0, (NZ - 1) * BLK)], st_send.at[5])
+    settle(pr.at[pl.ds(0, PLANE - 1)], st_send.at[0])
+    settle(gz.at[pl.ds(0, NZ - 1)], st_send.at[1])
+    settle(gf.at[others], st_send.at[2])
+
+    @pl.when(root)
+    def _():
+        settle(pr.at[pl.ds(0, PLANE - 1)], st_send.at[3])
+
+    @pl.when(z == 0)
+    def _():
+        settle(gz.at[pl.ds(0, NZ - 1)], st_send.at[4])
+
+    settle(gf.at[others], st_send.at[5])
     settle(mr, st_send.at[6])
     settle(mz.at[pl.ds(0, NZ - 1)], st_send.at[7])
     settle(mr, st_send.at[8])
@@ -348,7 +358,8 @@
     rows, block = trailing.shape
     rows_total = block * lax.axis_size("space")
     vmem = pl.BlockSpec(memory_space=pltpu.VMEM)
-    hbm = pl.BlockSpec(memory_space=pl.ANY)
+    hbm = pl.BlockSpec(memory_space=pltpu.HBM)
+    anywhere = pl.BlockSpec(memory_space=pl.ANY)
 
     def buf(*shape):
         return pltpu.VMEM(shape, F32)
@@ -361,15 +372,15 @@
             jax.ShapeDtypeStruct((rows, width), F32),
         ),
         in_specs=[hbm, hbm],
-        out_specs=(hbm, vmem, vmem),
+        out_specs=(anywhere, vmem, vmem),
         scratch_shapes=[
             buf(NY, width, part),
             buf(NY, rows, part),
             buf(width, width),
-            buf(NZ - 1, BLK, width),
-            buf(PLANE, BLK, width),
+            buf(PLANE, PIECE, width),
+            buf(NZ, PIECE, width),
             buf(width, width),
-            buf(BLK, width),
+            buf(PIECE, width),
             buf(width, width),
             buf(rows, width),
             buf(PAIRS - 1, BLK, width),
@@ -387,7 +398,8 @@
         compiler_params=pltpu.CompilerParams(
             collective_id=0, has_side_effects=True, vmem_limit_bytes=40 * 2**20),
         name="reduce_factor",
-    )(panel, trailing)
+    )(pltpu.with_memory_space_constraint(panel, pltpu.HBM),
+      pltpu.with_memory_space_constraint(trailing, pltpu.HBM))
 
     upper_factor, updated = pl.pallas_call(
         functools.partial(update_kernel, -1.0 / math.sqrt(rows_total)),

time: 92.7 us -> 74 us (0.80)
  Pallas kernels: 89.1 us -> 73.2 us
  local copies, waits for them, and re-layouts: 2.74 us -> 0.01 us
    pallas_call x1, Pallas kernels: 86.3 us -> 70.3 us  [per_device(): pl.pallas_call(main_kernel, out_shape=(jax.ShapeDtypeStruct((NY, width, p...]
    unnamed x6 -> x2, local copies, waits for them, and re-layouts: 2.74 us -> 0.01 us
where the time goes in v2:
time: 74 us; the launch traced here: 73.8 us
  Pallas kernels  73.2 us (99%)
    pallas_call x1, Pallas kernels, per_device(): pl.pallas_call(main_kernel, out_shape=(jax.ShapeDtypeStruct((NY, width, p...  70.3 us
    pallas_call x1, Pallas kernels, per_device(): pl.pallas_call(functools.partial(update_kernel, -1.0 / math.sqrt(rows_tot...  2.84 us

profile of v2, /device:TPU:1, one launch (start us, length us, event | category | flops | bytes accessed | tf_op | source)
XLA Modules:
  0.0 73.8 jit_solution(8107046427205553648)
XLA Ops:
  0.6 0.0 copy-start
  0.6 70.3 %reduce_factor.1 = (f32[4,128,1920]{2,1,0:T(8,128)S(1)}, f32[128,128]{1,0:T(8,128)S(1)}, f32[64,128]{1,0:T(8,128)S(1)}) custom-call(f32[128,1920]{1,0:T(8,128)} %p_hbm.1, f32[64,7680]{1,0:T(8,128)} %t_ref.1), custom_call_target="tpu_custom_call" | custom-call | tf_op jit(solution)/shard_map/reduce_factor/pallas_call | solution.py:367
  71.0 0.0 copy-done
  71.0 2.8 %apply_update.1 = (f32[128,128]{1,0:T(8,128)}, f32[64,7680]{1,0:T(8,128)}) custom-call(f32[4,128,1920]{2,1,0:T(8,128)S(1)} %get-tuple-element.5.p_ref, f32[64,7680]{1,0:T(8,128)S(1)} %copy-done, f32[64,128]{1,0:T(8,128)S(1)} %get-tuple-element.6.zt_ref, f32[128,128]{1,0:T(8,128)S(1)} %get-tuple-element.7.upper_ref), custom_call_target="tpu_custom_call" | custom-call | tf_op jit(solution)/shard_map/apply_update/pallas_call | solution.py:404
Async XLA Ops:
  0.6 70.4 %copy-start = (f32[64,7680]{1,0:T(8,128)S(1)}, f32[64,7680]{1,0:T(8,128)}, u32[]{:S(2)}) copy-start(f32[64,7680]{1,0:T(8,128)} %t_ref.1) | copy-start | bytes 5898244

commit v3 on v2

--- a/solution.py
+++ b/solution.py
@@ -127,7 +127,7 @@
 
 def main_kernel(p_hbm, t_hbm, gat_out, upper, zt,
                 gat, tv, g_loc, pr, gz, gf, p1s, p1f, m_loc, mr, mz, zsum, work, work_t,
-                gp_send, gp_recv, loc, out_sem, st_send, st_recv):
+                gp_send, gp_recv, loc, out_sem, st_send, st_recv, ready):
     width, part = p_hbm.shape
     half = width // 2
     space = lax.axis_index("space")
@@ -172,51 +172,69 @@
 
     own = pltpu.make_async_copy(p_hbm, gat.at[y], loc.at[0])
     own.start()
-    loop(1, NZ, lambda d: greet(at_z((z + d) % NZ)))
+    greet(at_z((z + 1) % NZ))
+    greet(at_z((z + NZ - 1) % NZ))
     loop(1, PLANE, lambda d: greet(at_plane((plane + d) % PLANE)))
     own.wait()
+    high, low = split2(gat[y])
+    both = dot_nt(high, jnp.concatenate([high, low], axis=0))
+    cross = both[:, width:]
+    g_loc[...] = both[:, :width] + cross + cross.T
+    pl.semaphore_wait(barrier, PLANE + 1)
+
+    def announce(level, step):
+        for zz in ((z + step) % NZ, (z + NZ - step) % NZ):
+            pl.semaphore_signal(ready.at[level], inc=1, device_id=at_z(zz), device_id_type=MESH)
+
+    announce(0, 1)
+
+    def gather_copy(src, dst, index, target):
+        return pltpu.make_async_remote_copy(
+            src_ref=src, dst_ref=dst, send_sem=gp_send.at[index], recv_sem=gp_recv.at[index],
+            device_id=(space, target), device_id_type=MESH)
+
+    def share(start, size, index, target):
+        rows = pl.ds(start, size)
+        copy = gather_copy(p_hbm.at[rows], gat.at[y, rows], index, target)
+        copy.start()
+        return copy
+
+    head = 8
+    first, second = pl.ds(0, half), pl.ds(half, half)
+    ra0 = share(0, head, 6, right)
+    lb0 = share(half, head, 7, left)
+
+    def scatter(d):
+        q = (plane + d) % PLANE
+        send(g_loc.at[rows_of(q // NY, PIECE)], pr.at[plane], 0, at_plane(q))
+
+    loop(1, PLANE, scatter)
+
+    @pl.when(root)
+    def _():
+        loop(1, PLANE, lambda q: send(gat.at[0, rows_of(q // NY, PIECE), pl.ds(0, width)], p1s, 3,
+                                      at_plane(q)))
+        p1s[...] = gat[0, 0:PIECE, 0:width]
+
+    ra = share(head, half - head, 0, right)
+    lb = share(half + head, half - head, 1, left)
+    rb = share(half, half, 2, right)
+    la = share(0, half, 3, left)
     loads = [pltpu.make_async_copy(t_hbm.at[:, pl.ds(c * part, part)], tv.at[c], loc.at[1 + c])
              for c in range(NY)]
     for load in loads:
         load.start()
-    high, low = split2(gat[y])
-    both = dot_nt(high, jnp.concatenate([high, low], axis=0))
-    cross = both[:, width:]
-    g_loc[...] = both[:, :width] + cross + cross.T
-    pl.semaphore_wait(barrier, PLANE + NZ - 2)
-
-    def scatter(d):
-        q = (plane + d) % PLANE
-        send(g_loc.at[rows_of(q // NY, PIECE)], pr.at[plane], 0, at_plane(q))
-
-    loop(1, PLANE, scatter)
-
-    @pl.when(root)
-    def _():
-        loop(1, PLANE, lambda q: send(gat.at[0, rows_of(q // NY, PIECE), pl.ds(0, width)], p1s, 3,
-                                      at_plane(q)))
-        p1s[...] = gat[0, 0:PIECE, 0:width]
-
-    first, second = pl.ds(0, half), pl.ds(half, half)
-
-    def gather_copy(src, dst, index, target):
-        return pltpu.make_async_remote_copy(
-            src_ref=src, dst_ref=dst, send_sem=gp_send.at[index], recv_sem=gp_recv.at[index],
-            device_id=(space, target), device_id_type=MESH)
-
-    ra = gather_copy(p_hbm.at[first], gat.at[y, first], 0, right)
-    lb = gather_copy(p_hbm.at[second], gat.at[y, second], 1, left)
-    rb = gather_copy(p_hbm.at[second], gat.at[y, second], 2, right)
-    la = gather_copy(p_hbm.at[first], gat.at[y, first], 3, left)
-    for copy in (ra, lb, rb, la):
-        copy.start()
-
+    pl.semaphore_wait(ready.at[0], 2)
+    announce(1, 2)
     pr[plane] = g_loc[rows_of(pair, PIECE), :]
+    pl.semaphore_wait(ready.at[1], 2)
+    announce(2, 4)
     settle(pr.at[pl.ds(0, PLANE - 1)], st_recv.at[0])
     total = pr[0]
     for q in range(1, PLANE):
         total = total + pr[q]
     gz[z] = total
+    pl.semaphore_wait(ready.at[2], 2)
     loop(1, NZ, lambda d: send(gz.at[z], gz.at[z], 1, at_z((z + d) % NZ)))
 
     @pl.when((z == 0) & (plane > 0))
@@ -244,6 +262,15 @@
 
     m_loc[...] = products(y)
     outs = [put_out(y, 0)]
+
+    ra0.wait_recv()
+    ra.wait_recv()
+    fa = gather_copy(gat.at[left, first], gat.at[left, first], 4, right)
+    fa.start()
+    lb0.wait_recv()
+    lb.wait_recv()
+    fb = gather_copy(gat.at[right, second], gat.at[right, second], 5, left)
+    fb.start()
 
     settle(gz.at[pl.ds(0, NZ - 1)], st_recv.at[1])
     total = gz[0]
@@ -260,33 +287,26 @@
     p1f[mine, :] = p1s[...]
     loop(1, PAIRS, lambda d: send(p1f.at[mine], p1f.at[mine], 5, at_pair((pair + d) % PAIRS)))
 
-    ra.wait_recv()
-    fa = gather_copy(gat.at[left, first], gat.at[left, first], 4, right)
-    fa.start()
-    lb.wait_recv()
-    fb = gather_copy(gat.at[right, second], gat.at[right, second], 5, left)
-    fb.start()
-
     others = pl.ds(0, (PAIRS - 1) * PIECE)
     settle(gf.at[others], st_recv.at[2])
     work[...] = gf[...]
     loop(0, width // BLK, lambda k: chol_step(k, work, upper))
-    settle(p1f.at[others], st_recv.at[5])
-    work[...] = gf[...] + jnp.dot(p1f[...], upper[...], precision=HIGHEST, preferred_element_type=F32)
-    work_t[...] = work[...].T
-    loop(0, width // BLK, lambda k: inverse_step(k, work, work_t))
-
-    @pl.when(space == 0)
-    def _():
-        m_loc[...] += jnp.dot(tv[0, :, 0:width], upper[...], precision=HIGHEST,
-                              preferred_element_type=F32)
-
     rb.wait_recv()
     m_loc[...] += products(left)
     outs.append(put_out(left, 1))
     la.wait_recv()
     m_loc[...] += products(right)
     outs.append(put_out(right, 2))
+    settle(p1f.at[others], st_recv.at[5])
+    work[...] = gf[...] + jnp.dot(p1f[...], upper[...], precision=HIGHEST, preferred_element_type=F32)
+    work_t[...] = work[...].T
+    loop(0, width // BLK, lambda k: inverse_step(k, work, work_t))
+
+    @pl.when(space == 0)
+    def _():
+        m_loc[...] += jnp.dot(tv[0, :, 0:width], upper[...], precision=HIGHEST,
+                              preferred_element_type=F32)
+
     fa.wait_recv()
     fb.wait_recv()
     m_loc[...] += products(far)
@@ -310,7 +330,7 @@
     settle(zsum.at[pl.ds(0, (PAIRS - 1) * BLK)], st_recv.at[8])
     zt[...] = zsum[...]
 
-    for copy in (ra, lb, rb, la, fa, fb):
+    for copy in (ra0, lb0, ra, lb, rb, la, fa, fb):
         copy.wait_send()
     for copy in outs:
         copy.wait()
@@ -332,25 +352,31 @@
     settle(mr, st_send.at[8])
 
 
-def update_kernel(scale, p_ref, t_ref, zt_ref, upper_ref, up_ref, out_ref):
+def update_kernel(scale, p_ref, t_ref, zt_ref, upper_ref, up_ref, out_ref, new, out_sem):
     zt = zt_ref[...]
-    rows = zt.shape[0]
-    width = zt.shape[1]
+    rows, width = zt.shape
+    part = p_ref.shape[2]
     zh, zl = split2(zt)
-    ph, pl_ = split2(p_ref[0])
-    double = jnp.dot(jnp.concatenate([zh, zl], axis=0), ph, preferred_element_type=F32)
-    cross = jnp.dot(zh, pl_, preferred_element_type=F32)
-    out_ref[...] = t_ref[...] - (double[:rows] + (double[rows:] + cross))
-
-    @pl.when(pl.program_id(0) == 0)
-    def _():
-        up_ref[...] = upper_ref[...] * scale
-
-    @pl.when((pl.program_id(0) == 0) & (lax.axis_index("space") == 0))
-    def _():
-        out_ref[:, 0:width] -= lax.dot_general(
-            zt, upper_ref[...], (((1,), (1,)), ((), ())), precision=HIGHEST,
-            preferred_element_type=F32)
+    pair = jnp.concatenate([zh, zl], axis=0)
+    copies = []
+    for c in range(NY):
+        cols = pl.ds(c * part, part)
+        ph, pl_ = split2(p_ref[c])
+        double = jnp.dot(pair, ph, preferred_element_type=F32)
+        cross = jnp.dot(zh, pl_, preferred_element_type=F32)
+        new[c] = t_ref[:, cols] - (double[:rows] + (double[rows:] + cross))
+        if c == 0:
+            @pl.when(lax.axis_index("space") == 0)
+            def _():
+                new[0, :, 0:width] -= lax.dot_general(
+                    zt, upper_ref[...], (((1,), (1,)), ((), ())), precision=HIGHEST,
+                    preferred_element_type=F32)
+        copy = pltpu.make_async_copy(new.at[c], out_ref.at[:, cols], out_sem.at[c])
+        copy.start()
+        copies.append(copy)
+    up_ref[...] = upper_ref[...] * scale
+    for copy in copies:
+        copy.wait()
 
 
 def per_device(panel, trailing):
@@ -388,12 +414,13 @@
             buf(rows, width),
             buf(width, width),
             buf(width, width),
-            pltpu.SemaphoreType.DMA((6,)),
-            pltpu.SemaphoreType.DMA((6,)),
+            pltpu.SemaphoreType.DMA((8,)),
+            pltpu.SemaphoreType.DMA((8,)),
             pltpu.SemaphoreType.DMA((1 + NY,)),
             pltpu.SemaphoreType.DMA((NY,)),
             pltpu.SemaphoreType.DMA((9,)),
             pltpu.SemaphoreType.DMA((9,)),
+            pltpu.SemaphoreType.REGULAR((3,)),
         ],
         compiler_params=pltpu.CompilerParams(
             collective_id=0, has_side_effects=True, vmem_limit_bytes=40 * 2**20),
@@ -403,21 +430,13 @@
 
     upper_factor, updated = pl.pallas_call(
         functools.partial(update_kernel, -1.0 / math.sqrt(rows_total)),
-        grid=(NY,),
         out_shape=(
             jax.ShapeDtypeStruct((width, width), F32),
             jax.ShapeDtypeStruct((rows, block), F32),
         ),
-        in_specs=[
-            pl.BlockSpec((1, width, part), lambda i: (i, 0, 0)),
-            pl.BlockSpec((rows, part), lambda i: (0, i)),
-            pl.BlockSpec((rows, width), lambda i: (0, 0)),
-            pl.BlockSpec((width, width), lambda i: (0, 0)),
-        ],
-        out_specs=(
-            pl.BlockSpec((width, width), lambda i: (0, 0)),
-            pl.BlockSpec((rows, part), lambda i: (0, i)),
-        ),
+        in_specs=[vmem] * 4,
+        out_specs=(vmem, hbm),
+        scratch_shapes=[buf(NY, rows, part), pltpu.SemaphoreType.DMA((NY,))],
         compiler_params=pltpu.CompilerParams(vmem_limit_bytes=40 * 2**20),
         name="apply_update",
     )(gat, trailing, zt, upper)

time: 74 us -> 73.7 us (level)
  no operation moved by 1% of the time
where the time goes in v3:
time: 73.7 us; the launch traced here: 73.6 us
  Pallas kernels  72.9 us (99%)
    pallas_call x1, Pallas kernels, per_device(): pl.pallas_call(main_kernel, out_shape=(jax.ShapeDtypeStruct((NY, width, p...  70.4 us
    pallas_call x1, Pallas kernels, per_device(): pl.pallas_call(functools.partial(update_kernel, -1.0 / math.sqrt(rows_tot...  2.55 us

profile of v3, /device:TPU:1, one launch (start us, length us, event | category | flops | bytes accessed | tf_op | source)
XLA Modules:
  0.0 73.6 jit_solution(7196339642458002476)
XLA Ops:
  0.6 0.0 copy-start
  0.6 70.4 %reduce_factor.1 = (f32[4,128,1920]{2,1,0:T(8,128)S(1)}, f32[128,128]{1,0:T(8,128)S(1)}, f32[64,128]{1,0:T(8,128)S(1)}) custom-call(f32[128,1920]{1,0:T(8,128)} %p_hbm.1, f32[64,7680]{1,0:T(8,128)} %t_ref.1), custom_call_target="tpu_custom_call" | custom-call | tf_op jit(solution)/shard_map/reduce_factor/pallas_call | solution.py:393
  71.0 0.0 copy-done
  71.0 2.6 %apply_update.1 = (f32[128,128]{1,0:T(8,128)}, f32[64,7680]{1,0:T(8,128)}) custom-call(f32[4,128,1920]{2,1,0:T(8,128)S(1)} %get-tuple-element.5.p_ref, f32[64,7680]{1,0:T(8,128)S(1)} %copy-done, f32[64,128]{1,0:T(8,128)S(1)} %get-tuple-element.6.zt_ref, f32[128,128]{1,0:T(8,128)S(1)} %get-tuple-element.7.upper_ref), custom_call_target="tpu_custom_call" | custom-call | tf_op jit(solution)/shard_map/apply_update/pallas_call | solution.py:431
Async XLA Ops:
  0.6 70.4 %copy-start = (f32[64,7680]{1,0:T(8,128)S(1)}, f32[64,7680]{1,0:T(8,128)}, u32[]{:S(2)}) copy-start(f32[64,7680]{1,0:T(8,128)} %t_ref.1) | copy-start | bytes 5898244

commit v4 on v3

--- a/solution.py
+++ b/solution.py
@@ -13,7 +13,6 @@
 HIGHEST = lax.Precision.HIGHEST
 MESH = pl.DeviceIdType.MESH
 NX, NZ, NCORE, NY = 4, 16, 2, 4
-PLANE = NX * NY * NCORE
 PAIRS = NX * NCORE
 BLK = 8
 PIECE = 16
@@ -126,8 +125,8 @@
 
 
 def main_kernel(p_hbm, t_hbm, gat_out, upper, zt,
-                gat, tv, g_loc, pr, gz, gf, p1s, p1f, m_loc, mr, mz, zsum, work, work_t,
-                gp_send, gp_recv, loc, out_sem, st_send, st_recv, ready):
+                gat, tv, g_loc, pr, yr, gz, gf, p1w, p1s, p1f, m_loc, mr, mz, zsum, work, work_t,
+                gp_send, gp_recv, loc, out_sem, st_send, st_recv, p1_send, ready):
     width, part = p_hbm.shape
     half = width // 2
     space = lax.axis_index("space")
@@ -136,17 +135,14 @@
     z = (space // NCORE) % NZ
     x = space // (NCORE * NZ)
     pair = x * NCORE + core
-    plane = pair * NY + y
     right, left, far = (y + 1) % NY, (y + NY - 1) % NY, (y + 2) % NY
     root = (space == 0) & (y == 0)
 
     def at_z(zz):
         return (x * (NZ * NCORE) + zz * NCORE + core, y)
 
-    def at_plane(q):
-        px = q // (NCORE * NY)
-        pc = (q // NY) % NCORE
-        return (px * (NZ * NCORE) + z * NCORE + pc, q % NY)
+    def at_y(yy):
+        return (space, yy)
 
     def at_pair(q):
         return ((q // NCORE) * (NZ * NCORE) + z * NCORE + q % NCORE, y)
@@ -174,13 +170,14 @@
     own.start()
     greet(at_z((z + 1) % NZ))
     greet(at_z((z + NZ - 1) % NZ))
-    loop(1, PLANE, lambda d: greet(at_plane((plane + d) % PLANE)))
+    loop(1, NY, lambda d: greet(at_y((y + d) % NY)))
+    loop(1, PAIRS, lambda d: greet(at_pair((pair + d) % PAIRS)))
     own.wait()
     high, low = split2(gat[y])
     both = dot_nt(high, jnp.concatenate([high, low], axis=0))
     cross = both[:, width:]
     g_loc[...] = both[:, :width] + cross + cross.T
-    pl.semaphore_wait(barrier, PLANE + 1)
+    pl.semaphore_wait(barrier, PAIRS + NY)
 
     def announce(level, step):
         for zz in ((z + step) % NZ, (z + NZ - step) % NZ):
@@ -199,23 +196,29 @@
         copy.start()
         return copy
 
-    head = 8
+    loop(1, PAIRS, lambda d: send(g_loc.at[rows_of((pair + d) % PAIRS, PIECE)], pr.at[d - 1], 0,
+                                  at_pair((pair + d) % PAIRS)))
+    head = 24
     first, second = pl.ds(0, half), pl.ds(half, half)
     ra0 = share(0, head, 6, right)
     lb0 = share(half, head, 7, left)
-
-    def scatter(d):
-        q = (plane + d) % PLANE
-        send(g_loc.at[rows_of(q // NY, PIECE)], pr.at[plane], 0, at_plane(q))
-
-    loop(1, PLANE, scatter)
+    pl.semaphore_wait(ready.at[0], 2)
+    announce(1, 2)
 
     @pl.when(root)
     def _():
-        loop(1, PLANE, lambda q: send(gat.at[0, rows_of(q // NY, PIECE), pl.ds(0, width)], p1s, 3,
-                                      at_plane(q)))
-        p1s[...] = gat[0, 0:PIECE, 0:width]
-
+        for d in range(1, NY):
+            pltpu.make_async_remote_copy(
+                src_ref=gat.at[0, :, pl.ds(0, width)], dst_ref=p1w, send_sem=p1_send.at[d - 1],
+                recv_sem=st_recv.at[3], device_id=at_y(d), device_id_type=MESH).start()
+        p1w[...] = gat[0, :, 0:width]
+
+    settle(pr, st_recv.at[0])
+    total = g_loc[rows_of(pair, PIECE), :]
+    for d in range(PAIRS - 1):
+        total = total + pr[d]
+    yr[y] = total
+    loop(1, NY, lambda d: send(yr.at[y], yr.at[y], 10, at_y((y + d) % NY)))
     ra = share(head, half - head, 0, right)
     lb = share(half + head, half - head, 1, left)
     rb = share(half, half, 2, right)
@@ -224,26 +227,32 @@
              for c in range(NY)]
     for load in loads:
         load.start()
-    pl.semaphore_wait(ready.at[0], 2)
-    announce(1, 2)
-    pr[plane] = g_loc[rows_of(pair, PIECE), :]
     pl.semaphore_wait(ready.at[1], 2)
     announce(2, 4)
-    settle(pr.at[pl.ds(0, PLANE - 1)], st_recv.at[0])
-    total = pr[0]
-    for q in range(1, PLANE):
-        total = total + pr[q]
+    settle(yr.at[pl.ds(0, NY - 1)], st_recv.at[10])
+    total = yr[0]
+    for q in range(1, NY):
+        total = total + yr[q]
     gz[z] = total
     pl.semaphore_wait(ready.at[2], 2)
     loop(1, NZ, lambda d: send(gz.at[z], gz.at[z], 1, at_z((z + d) % NZ)))
 
-    @pl.when((z == 0) & (plane > 0))
-    def _():
-        settle(p1s, st_recv.at[3])
+    @pl.when((space == 0) & (y > 0))
+    def _():
+        settle(p1w, st_recv.at[3])
+
+    @pl.when(space == 0)
+    def _():
+        loop(1, PAIRS, lambda q: send(p1w.at[rows_of(q, PIECE)], p1s, 4, at_pair(q)))
+        p1s[...] = p1w[0:PIECE, :]
+
+    @pl.when((z == 0) & (pair > 0))
+    def _():
+        settle(p1s, st_recv.at[4])
 
     @pl.when(z == 0)
     def _():
-        loop(1, NZ, lambda d: send(p1s, p1s, 4, at_z(d)))
+        loop(1, NZ, lambda d: send(p1s, p1s, 5, at_z(d)))
 
     for load in loads:
         load.wait()
@@ -282,10 +291,10 @@
 
     @pl.when(z > 0)
     def _():
-        settle(p1s, st_recv.at[4])
+        settle(p1s, st_recv.at[5])
 
     p1f[mine, :] = p1s[...]
-    loop(1, PAIRS, lambda d: send(p1f.at[mine], p1f.at[mine], 5, at_pair((pair + d) % PAIRS)))
+    loop(1, PAIRS, lambda d: send(p1f.at[mine], p1f.at[mine], 6, at_pair((pair + d) % PAIRS)))
 
     others = pl.ds(0, (PAIRS - 1) * PIECE)
     settle(gf.at[others], st_recv.at[2])
@@ -297,7 +306,7 @@
     la.wait_recv()
     m_loc[...] += products(right)
     outs.append(put_out(right, 2))
-    settle(p1f.at[others], st_recv.at[5])
+    settle(p1f.at[others], st_recv.at[6])
     work[...] = gf[...] + jnp.dot(p1f[...], upper[...], precision=HIGHEST, preferred_element_type=F32)
     work_t[...] = work[...].T
     loop(0, width // BLK, lambda k: inverse_step(k, work, work_t))
@@ -312,44 +321,50 @@
     m_loc[...] += products(far)
     outs.append(put_out(far, 3))
 
-    loop(1, PAIRS, lambda d: send(m_loc.at[rows_of((pair + d) % PAIRS, BLK)], mr.at[d - 1], 6,
+    loop(1, PAIRS, lambda d: send(m_loc.at[rows_of((pair + d) % PAIRS, BLK)], mr.at[d - 1], 7,
                                   at_pair((pair + d) % PAIRS)))
-    settle(mr, st_recv.at[6])
+    settle(mr, st_recv.at[7])
     tile = rows_of(pair, BLK)
     total = m_loc[tile, :]
     for d in range(PAIRS - 1):
         total = total + mr[d]
     mz[z] = total
-    loop(1, NZ, lambda d: send(mz.at[z], mz.at[z], 7, at_z((z + d) % NZ)))
-    settle(mz.at[pl.ds(0, NZ - 1)], st_recv.at[7])
+    loop(1, NZ, lambda d: send(mz.at[z], mz.at[z], 8, at_z((z + d) % NZ)))
+    settle(mz.at[pl.ds(0, NZ - 1)], st_recv.at[8])
     total = mz[0]
     for q in range(1, NZ):
         total = total + mz[q]
     zsum[tile, :] = jnp.dot(total, work[...], precision=HIGHEST, preferred_element_type=F32)
-    loop(1, PAIRS, lambda d: send(zsum.at[tile], zsum.at[tile], 8, at_pair((pair + d) % PAIRS)))
-    settle(zsum.at[pl.ds(0, (PAIRS - 1) * BLK)], st_recv.at[8])
+    loop(1, PAIRS, lambda d: send(zsum.at[tile], zsum.at[tile], 9, at_pair((pair + d) % PAIRS)))
+    settle(zsum.at[pl.ds(0, (PAIRS - 1) * BLK)], st_recv.at[9])
     zt[...] = zsum[...]
 
     for copy in (ra0, lb0, ra, lb, rb, la, fa, fb):
         copy.wait_send()
     for copy in outs:
         copy.wait()
-    settle(pr.at[pl.ds(0, PLANE - 1)], st_send.at[0])
+    settle(pr, st_send.at[0])
     settle(gz.at[pl.ds(0, NZ - 1)], st_send.at[1])
     settle(gf.at[others], st_send.at[2])
 
     @pl.when(root)
     def _():
-        settle(pr.at[pl.ds(0, PLANE - 1)], st_send.at[3])
+        for d in range(1, NY):
+            settle(p1w, p1_send.at[d - 1])
+
+    @pl.when(space == 0)
+    def _():
+        settle(gf.at[others], st_send.at[4])
 
     @pl.when(z == 0)
     def _():
-        settle(gz.at[pl.ds(0, NZ - 1)], st_send.at[4])
-
-    settle(gf.at[others], st_send.at[5])
-    settle(mr, st_send.at[6])
-    settle(mz.at[pl.ds(0, NZ - 1)], st_send.at[7])
-    settle(mr, st_send.at[8])
+        settle(gz.at[pl.ds(0, NZ - 1)], st_send.at[5])
+
+    settle(gf.at[others], st_send.at[6])
+    settle(mr, st_send.at[7])
+    settle(mz.at[pl.ds(0, NZ - 1)], st_send.at[8])
+    settle(mr, st_send.at[9])
+    settle(yr.at[pl.ds(0, NY - 1)], st_send.at[10])
 
 
 def update_kernel(scale, p_ref, t_ref, zt_ref, upper_ref, up_ref, out_ref, new, out_sem):
@@ -403,8 +418,10 @@
             buf(NY, width, part),
             buf(NY, rows, part),
             buf(width, width),
-            buf(PLANE, PIECE, width),
+            buf(PAIRS - 1, PIECE, width),
+            buf(NY, PIECE, width),
             buf(NZ, PIECE, width),
+            buf(width, width),
             buf(width, width),
             buf(PIECE, width),
             buf(width, width),
@@ -418,8 +435,9 @@
             pltpu.SemaphoreType.DMA((8,)),
             pltpu.SemaphoreType.DMA((1 + NY,)),
             pltpu.SemaphoreType.DMA((NY,)),
-            pltpu.SemaphoreType.DMA((9,)),
-            pltpu.SemaphoreType.DMA((9,)),
+            pltpu.SemaphoreType.DMA((11,)),
+            pltpu.SemaphoreType.DMA((11,)),
+            pltpu.SemaphoreType.DMA((NY - 1,)),
             pltpu.SemaphoreType.REGULAR((3,)),
         ],
         compiler_params=pltpu.CompilerParams(

time: 73.7 us -> 69.3 us (0.940)
  Pallas kernels: 72.9 us -> 68.5 us
    pallas_call x1, Pallas kernels: 70.4 us -> 66 us  [per_device(): pl.pallas_call(main_kernel, out_shape=(jax.ShapeDtypeStruct((NY, width, p...]
where the time goes in v4:
time: 69.3 us; the launch traced here: 69.2 us
  Pallas kernels  68.5 us (99%)
    pallas_call x1, Pallas kernels, per_device(): pl.pallas_call(main_kernel, out_shape=(jax.ShapeDtypeStruct((NY, width, p...  66 us
    pallas_call x1, Pallas kernels, per_device(): pl.pallas_call(functools.partial(update_kernel, -1.0 / math.sqrt(rows_tot...  2.55 us

profile of v4, /device:TPU:1, one launch (start us, length us, event | category | flops | bytes accessed | tf_op | source)
XLA Modules:
  0.0 69.2 jit_solution(4065161420495362817)
XLA Ops:
  0.6 0.0 copy-start
  0.6 66.0 %reduce_factor.1 = (f32[4,128,1920]{2,1,0:T(8,128)S(1)}, f32[128,128]{1,0:T(8,128)S(1)}, f32[64,128]{1,0:T(8,128)S(1)}) custom-call(f32[128,1920]{1,0:T(8,128)} %p_hbm.1, f32[64,7680]{1,0:T(8,128)} %t_ref.1), custom_call_target="tpu_custom_call" | custom-call | tf_op jit(solution)/shard_map/reduce_factor/pallas_call | solution.py:408
  66.6 0.0 copy-done
  66.6 2.6 %apply_update.1 = (f32[128,128]{1,0:T(8,128)}, f32[64,7680]{1,0:T(8,128)}) custom-call(f32[4,128,1920]{2,1,0:T(8,128)S(1)} %get-tuple-element.5.p_ref, f32[64,7680]{1,0:T(8,128)S(1)} %copy-done, f32[64,128]{1,0:T(8,128)S(1)} %get-tuple-element.6.zt_ref, f32[128,128]{1,0:T(8,128)S(1)} %get-tuple-element.7.upper_ref), custom_call_target="tpu_custom_call" | custom-call | tf_op jit(solution)/shard_map/apply_update/pallas_call | solution.py:449
Async XLA Ops:
  0.6 66.0 %copy-start = (f32[64,7680]{1,0:T(8,128)S(1)}, f32[64,7680]{1,0:T(8,128)}, u32[]{:S(2)}) copy-start(f32[64,7680]{1,0:T(8,128)} %t_ref.1) | copy-start | bytes 5898244

commit v5 on v4

--- a/solution.py
+++ b/solution.py
@@ -15,7 +15,10 @@
 NX, NZ, NCORE, NY = 4, 16, 2, 4
 PAIRS = NX * NCORE
 BLK = 8
+LANES = 128
 PIECE = 16
+EARLY = 10
+PLANE = PAIRS * NY
 
 
 def split2(x):
@@ -125,21 +128,28 @@
 
 
 def main_kernel(p_hbm, t_hbm, gat_out, upper, zt,
-                gat, tv, g_loc, pr, yr, gz, gf, p1w, p1s, p1f, m_loc, mr, mz, zsum, work, work_t,
+                gat, tv, tb, g_loc, pr, yr, gz, gf, p1w, p1s, p1f, m_loc, pm, mz, zsum, work, work_t,
                 gp_send, gp_recv, loc, out_sem, st_send, st_recv, p1_send, ready):
     width, part = p_hbm.shape
     half = width // 2
+    rows = t_hbm.shape[0]
+    tail = tb.shape[2]
+    main = part - tail
     space = lax.axis_index("space")
     y = lax.axis_index("col")
     core = space % NCORE
     z = (space // NCORE) % NZ
     x = space // (NCORE * NZ)
     pair = x * NCORE + core
+    plane = pair * NY + y
     right, left, far = (y + 1) % NY, (y + NY - 1) % NY, (y + 2) % NY
     root = (space == 0) & (y == 0)
 
     def at_z(zz):
         return (x * (NZ * NCORE) + zz * NCORE + core, y)
+
+    def at_plane(q):
+        return at_pair(q // NY)[0], q % NY
 
     def at_y(yy):
         return (space, yy)
@@ -190,18 +200,25 @@
             src_ref=src, dst_ref=dst, send_sem=gp_send.at[index], recv_sem=gp_recv.at[index],
             device_id=(space, target), device_id_type=MESH)
 
-    def share(start, size, index, target):
-        rows = pl.ds(start, size)
-        copy = gather_copy(p_hbm.at[rows], gat.at[y, rows], index, target)
+    def share(start, size, cols, index, target):
+        lines = pl.ds(start, size)
+        copy = gather_copy(p_hbm.at[lines, cols], gat.at[y, lines, cols], index, target)
         copy.start()
         return copy
 
+    def forward(block, lines, cols, index, target):
+        ref = gat.at[block, lines, cols]
+        copy = gather_copy(ref, ref, index, target)
+        copy.start()
+        return copy
+
     loop(1, PAIRS, lambda d: send(g_loc.at[rows_of((pair + d) % PAIRS, PIECE)], pr.at[d - 1], 0,
                                   at_pair((pair + d) % PAIRS)))
-    head = 24
+    head = 32
     first, second = pl.ds(0, half), pl.ds(half, half)
-    ra0 = share(0, head, 6, right)
-    lb0 = share(half, head, 7, left)
+    cols_a, cols_b = pl.ds(0, main), pl.ds(main, tail)
+    ra0 = share(0, head, cols_a, 6, right)
+    lb0 = share(half, head, cols_a, 7, left)
     pl.semaphore_wait(ready.at[0], 2)
     announce(1, 2)
 
@@ -219,10 +236,15 @@
         total = total + pr[d]
     yr[y] = total
     loop(1, NY, lambda d: send(yr.at[y], yr.at[y], 10, at_y((y + d) % NY)))
-    ra = share(head, half - head, 0, right)
-    lb = share(half + head, half - head, 1, left)
-    rb = share(half, half, 2, right)
-    la = share(0, half, 3, left)
+    ra = share(head, half - head, cols_a, 0, right)
+    lb = share(half + head, half - head, cols_a, 1, left)
+    rb = share(half, half, cols_a, 2, right)
+    la = share(0, half, cols_a, 3, left)
+    swaps = []
+    for index, target in ((8, right), (9, left), (10, far)):
+        cols = pl.ds(pl.multiple_of(target * part + main, LANES), tail)
+        swaps.append(gather_copy(t_hbm.at[:, cols], tb.at[y], index, target))
+        swaps[-1].start()
     loads = [pltpu.make_async_copy(t_hbm.at[:, pl.ds(c * part, part)], tv.at[c], loc.at[1 + c])
              for c in range(NY)]
     for load in loads:
@@ -257,29 +279,34 @@
     for load in loads:
         load.wait()
 
-    def products(c):
-        ph, pl_ = split2(gat[c])
-        th, tl = split2(tv[c])
+    def products(trail, block):
+        ph, pl_ = split2(block)
+        th, tl = split2(trail)
         four = dot_nt(jnp.concatenate([th, tl], axis=0), jnp.concatenate([ph, pl_], axis=0))
-        rows = th.shape[0]
-        return (four[:rows, :width] + four[rows:, :width]) + (four[:rows, width:] + four[rows:, width:])
-
-    def put_out(c, index):
-        copy = pltpu.make_async_copy(gat.at[c], gat_out.at[c], out_sem.at[index])
+        n = th.shape[0]
+        return (four[:n, :width] + four[n:, :width]) + (four[:n, width:] + four[n:, width:])
+
+    outs = []
+
+    def put_out(c, cols):
+        copy = pltpu.make_async_copy(gat.at[c, :, cols], gat_out.at[c, :, cols],
+                                     out_sem.at[len(outs)])
         copy.start()
-        return copy
-
-    m_loc[...] = products(y)
-    outs = [put_out(y, 0)]
+        outs.append(copy)
+
+    def add_main(c):
+        m_loc[0] += products(tv[c, :, 0:main], gat[c, :, 0:main])
+        put_out(c, cols_a)
+
+    m_loc[0] = products(tv[y], gat[y])
+    put_out(y, pl.ds(0, part))
 
     ra0.wait_recv()
     ra.wait_recv()
-    fa = gather_copy(gat.at[left, first], gat.at[left, first], 4, right)
-    fa.start()
+    fa = forward(left, first, cols_a, 4, right)
     lb0.wait_recv()
     lb.wait_recv()
-    fb = gather_copy(gat.at[right, second], gat.at[right, second], 5, left)
-    fb.start()
+    fb = forward(right, second, cols_a, 5, left)
 
     settle(gz.at[pl.ds(0, NZ - 1)], st_recv.at[1])
     total = gz[0]
@@ -301,35 +328,51 @@
     work[...] = gf[...]
     loop(0, width // BLK, lambda k: chol_step(k, work, upper))
     rb.wait_recv()
-    m_loc[...] += products(left)
-    outs.append(put_out(left, 1))
+    add_main(left)
     la.wait_recv()
-    m_loc[...] += products(right)
-    outs.append(put_out(right, 2))
+    add_main(right)
     settle(p1f.at[others], st_recv.at[6])
     work[...] = gf[...] + jnp.dot(p1f[...], upper[...], precision=HIGHEST, preferred_element_type=F32)
     work_t[...] = work[...].T
-    loop(0, width // BLK, lambda k: inverse_step(k, work, work_t))
+    loop(0, EARLY, lambda k: inverse_step(k, work, work_t))
 
     @pl.when(space == 0)
     def _():
-        m_loc[...] += jnp.dot(tv[0, :, 0:width], upper[...], precision=HIGHEST,
-                              preferred_element_type=F32)
-
+        m_loc[0] += jnp.dot(tv[0, :, 0:width], upper[...], precision=HIGHEST,
+                            preferred_element_type=F32)
+
+    for swap in swaps:
+        swap.wait_recv()
+    others_t = jnp.concatenate([tb[right], tb[far], tb[left]], axis=0)
+    swapped = products(others_t, gat[y, :, main:part])
+    for r in range(1, NY):
+        m_loc[r] = swapped[(r - 1) * rows:r * rows, :]
     fa.wait_recv()
     fb.wait_recv()
-    m_loc[...] += products(far)
-    outs.append(put_out(far, 3))
-
-    loop(1, PAIRS, lambda d: send(m_loc.at[rows_of((pair + d) % PAIRS, BLK)], mr.at[d - 1], 7,
-                                  at_pair((pair + d) % PAIRS)))
-    settle(mr, st_recv.at[7])
+    add_main(far)
+
+    def scatter(d):
+        q = (plane + d) % PLANE
+        ahead = (q % NY - y + NY) % NY
+        send(m_loc.at[ahead, rows_of(q // NY, BLK)], pm.at[d - 1], 7, at_plane(q))
+
+    loop(1, PLANE, scatter)
+    ra_b = share(0, half, cols_b, 11, right)
+    lb_b = share(half, half, cols_b, 12, left)
+    rb_b = share(half, half, cols_b, 13, right)
+    la_b = share(0, half, cols_b, 14, left)
+    loop(EARLY, width // BLK, lambda k: inverse_step(k, work, work_t))
+    settle(pm, st_recv.at[7])
     tile = rows_of(pair, BLK)
-    total = m_loc[tile, :]
-    for d in range(PAIRS - 1):
-        total = total + mr[d]
+    total = m_loc[0, tile, :]
+    for d in range(PLANE - 1):
+        total = total + pm[d]
     mz[z] = total
     loop(1, NZ, lambda d: send(mz.at[z], mz.at[z], 8, at_z((z + d) % NZ)))
+    ra_b.wait_recv()
+    fa_b = forward(left, first, cols_b, 15, right)
+    lb_b.wait_recv()
+    fb_b = forward(right, second, cols_b, 16, left)
     settle(mz.at[pl.ds(0, NZ - 1)], st_recv.at[8])
     total = mz[0]
     for q in range(1, NZ):
@@ -338,8 +381,15 @@
     loop(1, PAIRS, lambda d: send(zsum.at[tile], zsum.at[tile], 9, at_pair((pair + d) % PAIRS)))
     settle(zsum.at[pl.ds(0, (PAIRS - 1) * BLK)], st_recv.at[9])
     zt[...] = zsum[...]
-
-    for copy in (ra0, lb0, ra, lb, rb, la, fa, fb):
+    rb_b.wait_recv()
+    put_out(left, cols_b)
+    la_b.wait_recv()
+    put_out(right, cols_b)
+    fa_b.wait_recv()
+    fb_b.wait_recv()
+    put_out(far, cols_b)
+
+    for copy in (ra0, lb0, ra, lb, rb, la, fa, fb, *swaps, ra_b, lb_b, rb_b, la_b, fa_b, fb_b):
         copy.wait_send()
     for copy in outs:
         copy.wait()
@@ -361,9 +411,9 @@
         settle(gz.at[pl.ds(0, NZ - 1)], st_send.at[5])
 
     settle(gf.at[others], st_send.at[6])
-    settle(mr, st_send.at[7])
+    settle(pm, st_send.at[7])
     settle(mz.at[pl.ds(0, NZ - 1)], st_send.at[8])
-    settle(mr, st_send.at[9])
+    settle(zsum.at[pl.ds(0, (PAIRS - 1) * BLK)], st_send.at[9])
     settle(yr.at[pl.ds(0, NY - 1)], st_send.at[10])
 
 
@@ -397,6 +447,7 @@
 def per_device(panel, trailing):
     width, part = panel.shape
     rows, block = trailing.shape
+    tail = part // LANES * 2 // 5 * LANES
     rows_total = block * lax.axis_size("space")
     vmem = pl.BlockSpec(memory_space=pltpu.VMEM)
     hbm = pl.BlockSpec(memory_space=pltpu.HBM)
@@ -417,6 +468,7 @@
         scratch_shapes=[
             buf(NY, width, part),
             buf(NY, rows, part),
+            buf(NY, rows, tail),
             buf(width, width),
             buf(PAIRS - 1, PIECE, width),
             buf(NY, PIECE, width),
@@ -425,16 +477,16 @@
             buf(width, width),
             buf(PIECE, width),
             buf(width, width),
-            buf(rows, width),
-            buf(PAIRS - 1, BLK, width),
+            buf(NY, rows, width),
+            buf(PLANE - 1, BLK, width),
             buf(NZ, BLK, width),
             buf(rows, width),
             buf(width, width),
             buf(width, width),
-            pltpu.SemaphoreType.DMA((8,)),
-            pltpu.SemaphoreType.DMA((8,)),
+            pltpu.SemaphoreType.DMA((17,)),
+            pltpu.SemaphoreType.DMA((17,)),
             pltpu.SemaphoreType.DMA((1 + NY,)),
-            pltpu.SemaphoreType.DMA((NY,)),
+            pltpu.SemaphoreType.DMA((2 * NY - 1,)),
             pltpu.SemaphoreType.DMA((11,)),
             pltpu.SemaphoreType.DMA((11,)),
             pltpu.SemaphoreType.DMA((NY - 1,)),

time: 69.3 us -> 68 us (0.981)
  Pallas kernels: 68.5 us -> 67.2 us
    pallas_call x1, Pallas kernels: 66 us -> 64.7 us  [per_device(): pl.pallas_call(main_kernel, out_shape=(jax.ShapeDtypeStruct((NY, width, p...]
where the time goes in v5:
time: 68 us; the launch traced here: 67.9 us
  Pallas kernels  67.2 us (99%)
    pallas_call x1, Pallas kernels, per_device(): pl.pallas_call(main_kernel, out_shape=(jax.ShapeDtypeStruct((NY, width, p...  64.7 us
    pallas_call x1, Pallas kernels, per_device(): pl.pallas_call(functools.partial(update_kernel, -1.0 / math.sqrt(rows_tot...  2.55 us

profile of v5, /device:TPU:1, one launch (start us, length us, event | category | flops | bytes accessed | tf_op | source)
XLA Modules:
  0.0 67.9 jit_solution(7030554547945648357)
XLA Ops:
  0.6 0.0 copy-start
  0.6 64.7 %reduce_factor.1 = (f32[4,128,1920]{2,1,0:T(8,128)S(1)}, f32[128,128]{1,0:T(8,128)S(1)}, f32[64,128]{1,0:T(8,128)S(1)}) custom-call(f32[128,1920]{1,0:T(8,128)} %p_hbm.1, f32[64,7680]{1,0:T(8,128)} %t_ref.1), custom_call_target="tpu_custom_call" | custom-call | tf_op jit(solution)/shard_map/reduce_factor/pallas_call | solution.py:459
  65.3 0.0 copy-done
  65.3 2.6 %apply_update.1 = (f32[128,128]{1,0:T(8,128)}, f32[64,7680]{1,0:T(8,128)}) custom-call(f32[4,128,1920]{2,1,0:T(8,128)S(1)} %get-tuple-element.5.p_ref, f32[64,7680]{1,0:T(8,128)S(1)} %copy-done, f32[64,128]{1,0:T(8,128)S(1)} %get-tuple-element.6.zt_ref, f32[128,128]{1,0:T(8,128)S(1)} %get-tuple-element.7.upper_ref), custom_call_target="tpu_custom_call" | custom-call | tf_op jit(solution)/shard_map/apply_update/pallas_call | solution.py:501
Async XLA Ops:
  0.6 64.7 %copy-start = (f32[64,7680]{1,0:T(8,128)S(1)}, f32[64,7680]{1,0:T(8,128)}, u32[]{:S(2)}) copy-start(f32[64,7680]{1,0:T(8,128)} %t_ref.1) | copy-start | bytes 5898244

commit v6 on v5

--- a/solution.py
+++ b/solution.py
@@ -17,7 +17,7 @@
 BLK = 8
 LANES = 128
 PIECE = 16
-EARLY = 10
+EARLY, MIDDLE = 5, 12
 PLANE = PAIRS * NY
 
 
@@ -141,15 +141,29 @@
     z = (space // NCORE) % NZ
     x = space // (NCORE * NZ)
     pair = x * NCORE + core
-    plane = pair * NY + y
     right, left, far = (y + 1) % NY, (y + NY - 1) % NY, (y + 2) % NY
     root = (space == 0) & (y == 0)
 
+    z_order = sorted(range(1, NZ), key=lambda d: -min(d, NZ - d))
+    plane_order = sorted(
+        ((dx, dc, dy) for dx in range(NX) for dc in range(NCORE) for dy in range(NY)),
+        key=lambda d: -(min(d[0], NX - d[0]) + d[1] + min(d[2], NY - d[2])))[:-1]
+    pair_order = [(dx, dc) for dx, dc, dy in plane_order if dy == 0]
+
+    def pair_at(dx, dc):
+        return ((x + dx) % NX) * NCORE + (core + dc) % NCORE
+
+    def to_pairs(src, dst, stage):
+        for n, (dx, dc) in enumerate(pair_order):
+            q = pair_at(dx, dc)
+            send(src(q), dst(n), stage, at_pair(q))
+
+    def to_z(ref, stage):
+        for d in z_order:
+            send(ref, ref, stage, at_z((z + d) % NZ))
+
     def at_z(zz):
         return (x * (NZ * NCORE) + zz * NCORE + core, y)
-
-    def at_plane(q):
-        return at_pair(q // NY)[0], q % NY
 
     def at_y(yy):
         return (space, yy)
@@ -182,43 +196,42 @@
     greet(at_z((z + NZ - 1) % NZ))
     loop(1, NY, lambda d: greet(at_y((y + d) % NY)))
     loop(1, PAIRS, lambda d: greet(at_pair((pair + d) % PAIRS)))
+    pl.semaphore_wait(barrier, PAIRS + NY)
+
+    def announce(level, step):
+        for zz in ((z + step) % NZ, (z + NZ - step) % NZ):
+            pl.semaphore_signal(ready.at[level], inc=1, device_id=at_z(zz), device_id_type=MESH)
+
+    announce(0, 1)
+
+    def gather_copy(src, dst, index, target):
+        return pltpu.make_async_remote_copy(
+            src_ref=src, dst_ref=dst, send_sem=gp_send.at[index], recv_sem=gp_recv.at[index],
+            device_id=(space, target), device_id_type=MESH)
+
+    def share(start, size, cols, index, target):
+        lines = pl.ds(start, size)
+        copy = gather_copy(p_hbm.at[lines, cols], gat.at[y, lines, cols], index, target)
+        copy.start()
+        return copy
+
+    def forward(block, lines, cols, index, target):
+        ref = gat.at[block, lines, cols]
+        copy = gather_copy(ref, ref, index, target)
+        copy.start()
+        return copy
+
+    head = 48
+    first, second = pl.ds(0, half), pl.ds(half, half)
+    cols_a, cols_b = pl.ds(0, main), pl.ds(main, tail)
+    ra0 = share(0, head, cols_a, 6, right)
+    lb0 = share(half, head, cols_a, 7, left)
     own.wait()
     high, low = split2(gat[y])
     both = dot_nt(high, jnp.concatenate([high, low], axis=0))
     cross = both[:, width:]
     g_loc[...] = both[:, :width] + cross + cross.T
-    pl.semaphore_wait(barrier, PAIRS + NY)
-
-    def announce(level, step):
-        for zz in ((z + step) % NZ, (z + NZ - step) % NZ):
-            pl.semaphore_signal(ready.at[level], inc=1, device_id=at_z(zz), device_id_type=MESH)
-
-    announce(0, 1)
-
-    def gather_copy(src, dst, index, target):
-        return pltpu.make_async_remote_copy(
-            src_ref=src, dst_ref=dst, send_sem=gp_send.at[index], recv_sem=gp_recv.at[index],
-            device_id=(space, target), device_id_type=MESH)
-
-    def share(start, size, cols, index, target):
-        lines = pl.ds(start, size)
-        copy = gather_copy(p_hbm.at[lines, cols], gat.at[y, lines, cols], index, target)
-        copy.start()
-        return copy
-
-    def forward(block, lines, cols, index, target):
-        ref = gat.at[block, lines, cols]
-        copy = gather_copy(ref, ref, index, target)
-        copy.start()
-        return copy
-
-    loop(1, PAIRS, lambda d: send(g_loc.at[rows_of((pair + d) % PAIRS, PIECE)], pr.at[d - 1], 0,
-                                  at_pair((pair + d) % PAIRS)))
-    head = 32
-    first, second = pl.ds(0, half), pl.ds(half, half)
-    cols_a, cols_b = pl.ds(0, main), pl.ds(main, tail)
-    ra0 = share(0, head, cols_a, 6, right)
-    lb0 = share(half, head, cols_a, 7, left)
+    to_pairs(lambda q: g_loc.at[rows_of(q, PIECE)], lambda n: pr.at[n], 0)
     pl.semaphore_wait(ready.at[0], 2)
     announce(1, 2)
 
@@ -257,7 +270,7 @@
         total = total + yr[q]
     gz[z] = total
     pl.semaphore_wait(ready.at[2], 2)
-    loop(1, NZ, lambda d: send(gz.at[z], gz.at[z], 1, at_z((z + d) % NZ)))
+    to_z(gz.at[z], 1)
 
     @pl.when((space == 0) & (y > 0))
     def _():
@@ -314,14 +327,14 @@
         total = total + gz[q]
     mine = rows_of(pair, PIECE)
     gf[mine, :] = total
-    loop(1, PAIRS, lambda d: send(gf.at[mine], gf.at[mine], 2, at_pair((pair + d) % PAIRS)))
+    to_pairs(lambda q: gf.at[mine], lambda n: gf.at[mine], 2)
 
     @pl.when(z > 0)
     def _():
         settle(p1s, st_recv.at[5])
 
     p1f[mine, :] = p1s[...]
-    loop(1, PAIRS, lambda d: send(p1f.at[mine], p1f.at[mine], 6, at_pair((pair + d) % PAIRS)))
+    to_pairs(lambda q: p1f.at[mine], lambda n: p1f.at[mine], 6)
 
     others = pl.ds(0, (PAIRS - 1) * PIECE)
     settle(gf.at[others], st_recv.at[2])
@@ -351,24 +364,22 @@
     fb.wait_recv()
     add_main(far)
 
-    def scatter(d):
-        q = (plane + d) % PLANE
-        ahead = (q % NY - y + NY) % NY
-        send(m_loc.at[ahead, rows_of(q // NY, BLK)], pm.at[d - 1], 7, at_plane(q))
-
-    loop(1, PLANE, scatter)
+    for n, (dx, dc, dy) in enumerate(plane_order):
+        q = pair_at(dx, dc)
+        send(m_loc.at[dy, rows_of(q, BLK)], pm.at[n], 7, (at_pair(q)[0], (y + dy) % NY))
     ra_b = share(0, half, cols_b, 11, right)
     lb_b = share(half, half, cols_b, 12, left)
     rb_b = share(half, half, cols_b, 13, right)
     la_b = share(0, half, cols_b, 14, left)
-    loop(EARLY, width // BLK, lambda k: inverse_step(k, work, work_t))
+    loop(EARLY, MIDDLE, lambda k: inverse_step(k, work, work_t))
     settle(pm, st_recv.at[7])
     tile = rows_of(pair, BLK)
     total = m_loc[0, tile, :]
     for d in range(PLANE - 1):
         total = total + pm[d]
     mz[z] = total
-    loop(1, NZ, lambda d: send(mz.at[z], mz.at[z], 8, at_z((z + d) % NZ)))
+    to_z(mz.at[z], 8)
+    loop(MIDDLE, width // BLK, lambda k: inverse_step(k, work, work_t))
     ra_b.wait_recv()
     fa_b = forward(left, first, cols_b, 15, right)
     lb_b.wait_recv()
@@ -378,9 +389,7 @@
     for q in range(1, NZ):
         total = total + mz[q]
     zsum[tile, :] = jnp.dot(total, work[...], precision=HIGHEST, preferred_element_type=F32)
-    loop(1, PAIRS, lambda d: send(zsum.at[tile], zsum.at[tile], 9, at_pair((pair + d) % PAIRS)))
-    settle(zsum.at[pl.ds(0, (PAIRS - 1) * BLK)], st_recv.at[9])
-    zt[...] = zsum[...]
+    to_pairs(lambda q: zsum.at[tile], lambda n: zsum.at[tile], 9)
     rb_b.wait_recv()
     put_out(left, cols_b)
     la_b.wait_recv()
@@ -388,6 +397,8 @@
     fa_b.wait_recv()
     fb_b.wait_recv()
     put_out(far, cols_b)
+    settle(zsum.at[pl.ds(0, (PAIRS - 1) * BLK)], st_recv.at[9])
+    zt[...] = zsum[...]
 
     for copy in (ra0, lb0, ra, lb, rb, la, fa, fb, *swaps, ra_b, lb_b, rb_b, la_b, fa_b, fb_b):
         copy.wait_send()
@@ -422,14 +433,14 @@
     rows, width = zt.shape
     part = p_ref.shape[2]
     zh, zl = split2(zt)
-    pair = jnp.concatenate([zh, zl], axis=0)
+    quad = jnp.concatenate([jnp.concatenate([zh, zh], axis=1),
+                            jnp.concatenate([zl, zl], axis=1)], axis=0)
     copies = []
     for c in range(NY):
         cols = pl.ds(c * part, part)
         ph, pl_ = split2(p_ref[c])
-        double = jnp.dot(pair, ph, preferred_element_type=F32)
-        cross = jnp.dot(zh, pl_, preferred_element_type=F32)
-        new[c] = t_ref[:, cols] - (double[:rows] + (double[rows:] + cross))
+        both = jnp.dot(quad, jnp.concatenate([ph, pl_], axis=0), preferred_element_type=F32)
+        new[c] = t_ref[:, cols] - (both[:rows] + both[rows:])
         if c == 0:
             @pl.when(lax.axis_index("space") == 0)
             def _():

time: 68 us -> 65.1 us (0.957)
  Pallas kernels: 67.2 us -> 64.3 us
    pallas_call x1, Pallas kernels: 64.7 us -> 61.9 us  [per_device(): pl.pallas_call(main_kernel, out_shape=(jax.ShapeDtypeStruct((NY, width, p...]
where the time goes in v6:
time: 65.1 us; the launch traced here: 65 us
  Pallas kernels  64.3 us (99%)
    pallas_call x1, Pallas kernels, per_device(): pl.pallas_call(main_kernel, out_shape=(jax.ShapeDtypeStruct((NY, width, p...  61.9 us
    pallas_call x1, Pallas kernels, per_device(): pl.pallas_call(functools.partial(update_kernel, -1.0 / math.sqrt(rows_tot...  2.44 us

profile of v6, /device:TPU:1, one launch (start us, length us, event | category | flops | bytes accessed | tf_op | source)
XLA Modules:
  0.0 65.0 jit_solution(2779005879060197159)
XLA Ops:
  0.6 0.0 copy-start
  0.6 61.9 %reduce_factor.1 = (f32[4,128,1920]{2,1,0:T(8,128)S(1)}, f32[128,128]{1,0:T(8,128)S(1)}, f32[64,128]{1,0:T(8,128)S(1)}) custom-call(f32[128,1920]{1,0:T(8,128)} %p_hbm.1, f32[64,7680]{1,0:T(8,128)} %t_ref.1), custom_call_target="tpu_custom_call" | custom-call | tf_op jit(solution)/shard_map/reduce_factor/pallas_call | solution.py:470
  62.5 0.0 copy-done
  62.5 2.4 %apply_update.1 = (f32[128,128]{1,0:T(8,128)}, f32[64,7680]{1,0:T(8,128)}) custom-call(f32[4,128,1920]{2,1,0:T(8,128)S(1)} %get-tuple-element.5.p_ref, f32[64,7680]{1,0:T(8,128)S(1)} %copy-done, f32[64,128]{1,0:T(8,128)S(1)} %get-tuple-element.6.zt_ref, f32[128,128]{1,0:T(8,128)S(1)} %get-tuple-element.7.upper_ref), custom_call_target="tpu_custom_call" | custom-call | tf_op jit(solution)/shard_map/apply_update/pallas_call | solution.py:512
Async XLA Ops:
  0.6 61.9 %copy-start = (f32[64,7680]{1,0:T(8,128)S(1)}, f32[64,7680]{1,0:T(8,128)}, u32[]{:S(2)}) copy-start(f32[64,7680]{1,0:T(8,128)} %t_ref.1) | copy-start | bytes 5898244

commit v7 on v6

--- a/solution.py
+++ b/solution.py
@@ -194,15 +194,23 @@
     own.start()
     greet(at_z((z + 1) % NZ))
     greet(at_z((z + NZ - 1) % NZ))
-    loop(1, NY, lambda d: greet(at_y((y + d) % NY)))
-    loop(1, PAIRS, lambda d: greet(at_pair((pair + d) % PAIRS)))
-    pl.semaphore_wait(barrier, PAIRS + NY)
-
-    def announce(level, step):
-        for zz in ((z + step) % NZ, (z + NZ - step) % NZ):
-            pl.semaphore_signal(ready.at[level], inc=1, device_id=at_z(zz), device_id_type=MESH)
-
-    announce(0, 1)
+    for step in (1, NY - 1):
+        greet(at_y((y + step) % NY))
+    near = [(0, 1), (1, 0), (NX - 1, 0), (1, 1), (NX - 1, 1)]
+    for dx, dc in near:
+        greet(at_pair(pair_at(dx, dc)))
+    pl.semaphore_wait(barrier, 4 + len(near))
+
+    def announce(level, one, other):
+        for device in (one, other):
+            pl.semaphore_signal(ready.at[level], inc=1, device_id=device, device_id_type=MESH)
+
+    def announce_z(level, step):
+        announce(level, at_z((z + step) % NZ), at_z((z + NZ - step) % NZ))
+
+    announce(3, at_pair(pair_at(1, 0)), at_pair(pair_at(NX - 1, 0)))
+    announce(4, at_y(right), at_y(left))
+    announce_z(0, 1)
 
     def gather_copy(src, dst, index, target):
         return pltpu.make_async_remote_copy(
@@ -231,9 +239,11 @@
     both = dot_nt(high, jnp.concatenate([high, low], axis=0))
     cross = both[:, width:]
     g_loc[...] = both[:, :width] + cross + cross.T
+    pl.semaphore_wait(ready.at[3], 2)
     to_pairs(lambda q: g_loc.at[rows_of(q, PIECE)], lambda n: pr.at[n], 0)
     pl.semaphore_wait(ready.at[0], 2)
-    announce(1, 2)
+    announce_z(1, 2)
+    pl.semaphore_wait(ready.at[4], 2)
 
     @pl.when(root)
     def _():
@@ -263,7 +273,7 @@
     for load in loads:
         load.start()
     pl.semaphore_wait(ready.at[1], 2)
-    announce(2, 4)
+    announce_z(2, 4)
     settle(yr.at[pl.ds(0, NY - 1)], st_recv.at[10])
     total = yr[0]
     for q in range(1, NY):
@@ -320,6 +330,9 @@
     lb0.wait_recv()
     lb.wait_recv()
     fb = forward(right, second, cols_a, 5, left)
+    fill = 32
+    ra_b0 = share(0, fill, cols_b, 17, right)
+    lb_b0 = share(half, fill, cols_b, 18, left)
 
     settle(gz.at[pl.ds(0, NZ - 1)], st_recv.at[1])
     total = gz[0]
@@ -367,8 +380,8 @@
     for n, (dx, dc, dy) in enumerate(plane_order):
         q = pair_at(dx, dc)
         send(m_loc.at[dy, rows_of(q, BLK)], pm.at[n], 7, (at_pair(q)[0], (y + dy) % NY))
-    ra_b = share(0, half, cols_b, 11, right)
-    lb_b = share(half, half, cols_b, 12, left)
+    ra_b = share(fill, half - fill, cols_b, 11, right)
+    lb_b = share(half + fill, half - fill, cols_b, 12, left)
     rb_b = share(half, half, cols_b, 13, right)
     la_b = share(0, half, cols_b, 14, left)
     loop(EARLY, MIDDLE, lambda k: inverse_step(k, work, work_t))
@@ -380,8 +393,10 @@
     mz[z] = total
     to_z(mz.at[z], 8)
     loop(MIDDLE, width // BLK, lambda k: inverse_step(k, work, work_t))
+    ra_b0.wait_recv()
     ra_b.wait_recv()
     fa_b = forward(left, first, cols_b, 15, right)
+    lb_b0.wait_recv()
     lb_b.wait_recv()
     fb_b = forward(right, second, cols_b, 16, left)
     settle(mz.at[pl.ds(0, NZ - 1)], st_recv.at[8])
@@ -400,7 +415,7 @@
     settle(zsum.at[pl.ds(0, (PAIRS - 1) * BLK)], st_recv.at[9])
     zt[...] = zsum[...]
 
-    for copy in (ra0, lb0, ra, lb, rb, la, fa, fb, *swaps, ra_b, lb_b, rb_b, la_b, fa_b, fb_b):
+    for copy in (ra0, lb0, ra, lb, rb, la, fa, fb, *swaps, ra_b0, lb_b0, ra_b, lb_b, rb_b, la_b, fa_b, fb_b):
         copy.wait_send()
     for copy in outs:
         copy.wait()
@@ -428,14 +443,16 @@
     settle(yr.at[pl.ds(0, NY - 1)], st_send.at[10])
 
 
-def update_kernel(scale, p_ref, t_ref, zt_ref, upper_ref, up_ref, out_ref, new, out_sem):
+def update_kernel(scale, p_ref, t_ref, zt_ref, upper_ref, up_ref, out_ref, up, new, out_sem):
+    up[...] = upper_ref[...] * scale
+    copies = [pltpu.make_async_copy(up, up_ref, out_sem.at[NY])]
+    copies[0].start()
     zt = zt_ref[...]
     rows, width = zt.shape
     part = p_ref.shape[2]
     zh, zl = split2(zt)
     quad = jnp.concatenate([jnp.concatenate([zh, zh], axis=1),
                             jnp.concatenate([zl, zl], axis=1)], axis=0)
-    copies = []
     for c in range(NY):
         cols = pl.ds(c * part, part)
         ph, pl_ = split2(p_ref[c])
@@ -450,7 +467,6 @@
         copy = pltpu.make_async_copy(new.at[c], out_ref.at[:, cols], out_sem.at[c])
         copy.start()
         copies.append(copy)
-    up_ref[...] = upper_ref[...] * scale
     for copy in copies:
         copy.wait()
 
@@ -494,14 +510,14 @@
             buf(rows, width),
             buf(width, width),
             buf(width, width),
-            pltpu.SemaphoreType.DMA((17,)),
-            pltpu.SemaphoreType.DMA((17,)),
+            pltpu.SemaphoreType.DMA((19,)),
+            pltpu.SemaphoreType.DMA((19,)),
             pltpu.SemaphoreType.DMA((1 + NY,)),
             pltpu.SemaphoreType.DMA((2 * NY - 1,)),
             pltpu.SemaphoreType.DMA((11,)),
             pltpu.SemaphoreType.DMA((11,)),
             pltpu.SemaphoreType.DMA((NY - 1,)),
-            pltpu.SemaphoreType.REGULAR((3,)),
+            pltpu.SemaphoreType.REGULAR((5,)),
         ],
         compiler_params=pltpu.CompilerParams(
             collective_id=0, has_side_effects=True, vmem_limit_bytes=40 * 2**20),
@@ -516,8 +532,9 @@
             jax.ShapeDtypeStruct((rows, block), F32),
         ),
         in_specs=[vmem] * 4,
-        out_specs=(vmem, hbm),
-        scratch_shapes=[buf(NY, rows, part), pltpu.SemaphoreType.DMA((NY,))],
+        out_specs=(hbm, hbm),
+        scratch_shapes=[
+            buf(width, width), buf(NY, rows, part), pltpu.SemaphoreType.DMA((NY + 1,))],
         compiler_params=pltpu.CompilerParams(vmem_limit_bytes=40 * 2**20),
         name="apply_update",
     )(gat, trailing, zt, upper)

time: 65.1 us -> 64.9 us (level)
  no operation moved by 1% of the time
where the time goes in v7:
time: 64.9 us; the launch traced here: 64.8 us
  Pallas kernels  64.2 us (99%)
  between operations  0.65 us (1%)
    pallas_call x1, Pallas kernels, per_device(): pl.pallas_call(main_kernel, out_shape=(jax.ShapeDtypeStruct((NY, width, p...  62.4 us
    pallas_call x1, Pallas kernels, per_device(): pl.pallas_call(functools.partial(update_kernel, -1.0 / math.sqrt(rows_tot...  1.81 us

profile of v7, /device:TPU:1, one launch (start us, length us, event | category | flops | bytes accessed | tf_op | source)
XLA Modules:
  0.0 64.8 jit_solution(10736325531101235783)
XLA Ops:
  0.6 0.0 copy-start
  0.6 62.4 %reduce_factor.1 = (f32[4,128,1920]{2,1,0:T(8,128)S(1)}, f32[128,128]{1,0:T(8,128)S(1)}, f32[64,128]{1,0:T(8,128)S(1)}) custom-call(f32[128,1920]{1,0:T(8,128)} %p_hbm.1, f32[64,7680]{1,0:T(8,128)} %t_ref.1), custom_call_target="tpu_custom_call" | custom-call | tf_op jit(solution)/shard_map/reduce_factor/pallas_call | solution.py:486
  63.0 0.0 copy-done
  63.0 1.8 %apply_update.1 = (f32[128,128]{1,0:T(8,128)}, f32[64,7680]{1,0:T(8,128)}) custom-call(f32[4,128,1920]{2,1,0:T(8,128)S(1)} %get-tuple-element.5.p_ref, f32[64,7680]{1,0:T(8,128)S(1)} %copy-done, f32[64,128]{1,0:T(8,128)S(1)} %get-tuple-element.6.zt_ref, f32[128,128]{1,0:T(8,128)S(1)} %get-tuple-element.7.upper_ref), custom_call_target="tpu_custom_call" | custom-call | tf_op jit(solution)/shard_map/apply_update/pallas_call | solution.py:528
Async XLA Ops:
  0.6 62.4 %copy-start = (f32[64,7680]{1,0:T(8,128)S(1)}, f32[64,7680]{1,0:T(8,128)}, u32[]{:S(2)}) copy-start(f32[64,7680]{1,0:T(8,128)} %t_ref.1) | copy-start | bytes 5898244

commit v8 on v7

--- a/solution.py
+++ b/solution.py
@@ -17,7 +17,7 @@
 BLK = 8
 LANES = 128
 PIECE = 16
-EARLY, MIDDLE = 5, 12
+MIDDLE = 8
 PLANE = PAIRS * NY
 
 
@@ -127,8 +127,8 @@
     mat_t[...] = jnp.where(keep, mat_t[...], 0.0) - dot_tn(right, left)
 
 
-def main_kernel(p_hbm, t_hbm, gat_out, upper, zt,
-                gat, tv, tb, g_loc, pr, yr, gz, gf, p1w, p1s, p1f, m_loc, pm, mz, zsum, work, work_t,
+def main_kernel(p_hbm, t_hbm, gat_out, upper_out, zt,
+                gat, tv, tb, g_loc, pr, yr, gz, gf, p1w, p1s, p1f, upper, m_loc, pm, mz, zsum, work, work_t,
                 gp_send, gp_recv, loc, out_sem, st_send, st_recv, p1_send, ready):
     width, part = p_hbm.shape
     half = width // 2
@@ -229,11 +229,12 @@
         copy.start()
         return copy
 
-    head = 48
     first, second = pl.ds(0, half), pl.ds(half, half)
     cols_a, cols_b = pl.ds(0, main), pl.ds(main, tail)
-    ra0 = share(0, head, cols_a, 6, right)
-    lb0 = share(half, head, cols_a, 7, left)
+    ra = share(0, half, cols_a, 0, right)
+    lb = share(half, half, cols_a, 1, left)
+    rb = share(half, half, cols_a, 2, right)
+    la = share(0, half, cols_a, 3, left)
     own.wait()
     high, low = split2(gat[y])
     both = dot_nt(high, jnp.concatenate([high, low], axis=0))
@@ -259,10 +260,6 @@
         total = total + pr[d]
     yr[y] = total
     loop(1, NY, lambda d: send(yr.at[y], yr.at[y], 10, at_y((y + d) % NY)))
-    ra = share(head, half - head, cols_a, 0, right)
-    lb = share(half + head, half - head, cols_a, 1, left)
-    rb = share(half, half, cols_a, 2, right)
-    la = share(0, half, cols_a, 3, left)
     swaps = []
     for index, target in ((8, right), (9, left), (10, far)):
         cols = pl.ds(pl.multiple_of(target * part + main, LANES), tail)
@@ -324,15 +321,13 @@
     m_loc[0] = products(tv[y], gat[y])
     put_out(y, pl.ds(0, part))
 
-    ra0.wait_recv()
     ra.wait_recv()
     fa = forward(left, first, cols_a, 4, right)
-    lb0.wait_recv()
     lb.wait_recv()
     fb = forward(right, second, cols_a, 5, left)
-    fill = 32
-    ra_b0 = share(0, fill, cols_b, 17, right)
-    lb_b0 = share(half, fill, cols_b, 18, left)
+    fill = 24
+    ra_b0 = share(0, fill, cols_b, 6, right)
+    lb_b0 = share(half, fill, cols_b, 7, left)
 
     settle(gz.at[pl.ds(0, NZ - 1)], st_recv.at[1])
     total = gz[0]
@@ -353,15 +348,12 @@
     settle(gf.at[others], st_recv.at[2])
     work[...] = gf[...]
     loop(0, width // BLK, lambda k: chol_step(k, work, upper))
+    outs.append(pltpu.make_async_copy(upper, upper_out, out_sem.at[len(outs)]))
+    outs[-1].start()
     rb.wait_recv()
     add_main(left)
     la.wait_recv()
     add_main(right)
-    settle(p1f.at[others], st_recv.at[6])
-    work[...] = gf[...] + jnp.dot(p1f[...], upper[...], precision=HIGHEST, preferred_element_type=F32)
-    work_t[...] = work[...].T
-    loop(0, EARLY, lambda k: inverse_step(k, work, work_t))
-
     @pl.when(space == 0)
     def _():
         m_loc[0] += jnp.dot(tv[0, :, 0:width], upper[...], precision=HIGHEST,
@@ -384,7 +376,10 @@
     lb_b = share(half + fill, half - fill, cols_b, 12, left)
     rb_b = share(half, half, cols_b, 13, right)
     la_b = share(0, half, cols_b, 14, left)
-    loop(EARLY, MIDDLE, lambda k: inverse_step(k, work, work_t))
+    settle(p1f.at[others], st_recv.at[6])
+    work[...] = gf[...] + jnp.dot(p1f[...], upper[...], precision=HIGHEST, preferred_element_type=F32)
+    work_t[...] = work[...].T
+    loop(0, MIDDLE, lambda k: inverse_step(k, work, work_t))
     settle(pm, st_recv.at[7])
     tile = rows_of(pair, BLK)
     total = m_loc[0, tile, :]
@@ -415,7 +410,7 @@
     settle(zsum.at[pl.ds(0, (PAIRS - 1) * BLK)], st_recv.at[9])
     zt[...] = zsum[...]
 
-    for copy in (ra0, lb0, ra, lb, rb, la, fa, fb, *swaps, ra_b0, lb_b0, ra_b, lb_b, rb_b, la_b, fa_b, fb_b):
+    for copy in (ra, lb, rb, la, fa, fb, *swaps, ra_b0, lb_b0, ra_b, lb_b, rb_b, la_b, fa_b, fb_b):
         copy.wait_send()
     for copy in outs:
         copy.wait()
@@ -474,7 +469,7 @@
 def per_device(panel, trailing):
     width, part = panel.shape
     rows, block = trailing.shape
-    tail = part // LANES * 2 // 5 * LANES
+    tail = part // LANES * 11 // 15 * LANES
     rows_total = block * lax.axis_size("space")
     vmem = pl.BlockSpec(memory_space=pltpu.VMEM)
     hbm = pl.BlockSpec(memory_space=pltpu.HBM)
@@ -491,7 +486,7 @@
             jax.ShapeDtypeStruct((rows, width), F32),
         ),
         in_specs=[hbm, hbm],
-        out_specs=(anywhere, vmem, vmem),
+        out_specs=(anywhere, anywhere, vmem),
         scratch_shapes=[
             buf(NY, width, part),
             buf(NY, rows, part),
@@ -504,16 +499,17 @@
             buf(width, width),
             buf(PIECE, width),
             buf(width, width),
+            buf(width, width),
             buf(NY, rows, width),
             buf(PLANE - 1, BLK, width),
             buf(NZ, BLK, width),
             buf(rows, width),
             buf(width, width),
             buf(width, width),
-            pltpu.SemaphoreType.DMA((19,)),
-            pltpu.SemaphoreType.DMA((19,)),
+            pltpu.SemaphoreType.DMA((17,)),
+            pltpu.SemaphoreType.DMA((17,)),
             pltpu.SemaphoreType.DMA((1 + NY,)),
-            pltpu.SemaphoreType.DMA((2 * NY - 1,)),
+            pltpu.SemaphoreType.DMA((2 * NY,)),
             pltpu.SemaphoreType.DMA((11,)),
             pltpu.SemaphoreType.DMA((11,)),
             pltpu.SemaphoreType.DMA((NY - 1,)),

time: 64.9 us -> 69.9 us (1.077)
  Pallas kernels: 64.2 us -> 69.1 us
    pallas_call x1, Pallas kernels: 62.4 us -> 67.3 us  [per_device(): pl.pallas_call(main_kernel, out_shape=(jax.ShapeDtypeStruct((NY, width, p...]
where the time goes in v8:
time: 69.9 us; the launch traced here: 69.8 us
  Pallas kernels  69.1 us (99%)
    pallas_call x1, Pallas kernels, per_device(): pl.pallas_call(main_kernel, out_shape=(jax.ShapeDtypeStruct((NY, width, p...  67.3 us
    pallas_call x1, Pallas kernels, per_device(): pl.pallas_call(functools.partial(update_kernel, -1.0 / math.sqrt(rows_tot...  1.81 us

profile of v8, /device:TPU:1, one launch (start us, length us, event | category | flops | bytes accessed | tf_op | source)
XLA Modules:
  0.0 69.8 jit_solution(4075813159196208410)
XLA Ops:
  0.6 0.0 copy-start
  0.6 67.3 %reduce_factor.1 = (f32[4,128,1920]{2,1,0:T(8,128)S(1)}, f32[128,128]{1,0:T(8,128)S(1)}, f32[64,128]{1,0:T(8,128)S(1)}) custom-call(f32[128,1920]{1,0:T(8,128)} %p_hbm.1, f32[64,7680]{1,0:T(8,128)} %t_ref.1), custom_call_target="tpu_custom_call" | custom-call | tf_op jit(solution)/shard_map/reduce_factor/pallas_call | solution.py:481
  68.0 0.0 copy-done
  68.0 1.8 %apply_update.1 = (f32[128,128]{1,0:T(8,128)}, f32[64,7680]{1,0:T(8,128)}) custom-call(f32[4,128,1920]{2,1,0:T(8,128)S(1)} %get-tuple-element.5.p_ref, f32[64,7680]{1,0:T(8,128)S(1)} %copy-done, f32[64,128]{1,0:T(8,128)S(1)} %get-tuple-element.6.zt_ref, f32[128,128]{1,0:T(8,128)S(1)} %get-tuple-element.7.upper_ref), custom_call_target="tpu_custom_call" | custom-call | tf_op jit(solution)/shard_map/apply_update/pallas_call | solution.py:524
Async XLA Ops:
  0.6 67.4 %copy-start = (f32[64,7680]{1,0:T(8,128)S(1)}, f32[64,7680]{1,0:T(8,128)}, u32[]{:S(2)}) copy-start(f32[64,7680]{1,0:T(8,128)} %t_ref.1) | copy-start | bytes 5898244

commit v9 on v8

--- a/solution.py
+++ b/solution.py
@@ -18,6 +18,7 @@
 LANES = 128
 PIECE = 16
 MIDDLE = 8
+EARLY_PLANES = 7
 PLANE = PAIRS * NY
 
 
@@ -128,7 +129,7 @@
 
 
 def main_kernel(p_hbm, t_hbm, gat_out, upper_out, zt,
-                gat, tv, tb, g_loc, pr, yr, gz, gf, p1w, p1s, p1f, upper, m_loc, pm, mz, zsum, work, work_t,
+                gat, tv, tb, g_loc, pr, yr, gz, gf, p1w, p1s, p1f, t1, upper, m_loc, pm, mz, zsum, work, work_t,
                 gp_send, gp_recv, loc, out_sem, st_send, st_recv, p1_send, ready):
     width, part = p_hbm.shape
     half = width // 2
@@ -229,7 +230,7 @@
         copy.start()
         return copy
 
-    first, second = pl.ds(0, half), pl.ds(half, half)
+    top, bottom = pl.ds(0, half), pl.ds(half, half)
     cols_a, cols_b = pl.ds(0, main), pl.ds(main, tail)
     ra = share(0, half, cols_a, 0, right)
     lb = share(half, half, cols_a, 1, left)
@@ -299,6 +300,11 @@
     for load in loads:
         load.wait()
 
+    @pl.when(space == 0)
+    def _():
+        to_pairs(lambda q: tv.at[0, rows_of(q, BLK), pl.ds(0, width)], lambda n: t1, 11)
+        t1[...] = tv[0, 0:BLK, 0:width]
+
     def products(trail, block):
         ph, pl_ = split2(block)
         th, tl = split2(trail)
@@ -316,18 +322,67 @@
 
     def add_main(c):
         m_loc[0] += products(tv[c, :, 0:main], gat[c, :, 0:main])
-        put_out(c, cols_a)
 
     m_loc[0] = products(tv[y], gat[y])
     put_out(y, pl.ds(0, part))
 
     ra.wait_recv()
-    fa = forward(left, first, cols_a, 4, right)
+    fa = forward(left, top, cols_a, 4, right)
     lb.wait_recv()
-    fb = forward(right, second, cols_a, 5, left)
+    fb = forward(right, bottom, cols_a, 5, left)
     fill = 24
     ra_b0 = share(0, fill, cols_b, 6, right)
     lb_b0 = share(half, fill, cols_b, 7, left)
+
+    def second(start, size, index, target):
+        lines = pl.ds(start, size)
+        return gather_copy(p_hbm.at[lines, cols_b], gat.at[y, lines, cols_b], index, target)
+
+    def relay(block, lines, index, target):
+        ref = gat.at[block, lines, cols_b]
+        return gather_copy(ref, ref, index, target)
+
+    ra_b = second(fill, half - fill, 11, right)
+    lb_b = second(half + fill, half - fill, 12, left)
+    rb_b = second(half, half, 13, right)
+    la_b = second(0, half, 14, left)
+    fa_b = relay(left, top, 15, right)
+    fb_b = relay(right, bottom, 16, left)
+
+    def finish_first():
+        rb.wait_recv()
+        add_main(left)
+        la.wait_recv()
+        add_main(right)
+        for swap in swaps:
+            swap.wait_recv()
+        others_t = jnp.concatenate([tb[right], tb[far], tb[left]], axis=0)
+        swapped = products(others_t, gat[y, :, main:part])
+        for r in range(1, NY):
+            m_loc[r] = swapped[(r - 1) * rows:r * rows, :]
+        fa.wait_recv()
+        fb.wait_recv()
+        add_main(far)
+        for n, (dx, dc, dy) in enumerate(plane_order):
+            q = pair_at(dx, dc)
+            send(m_loc.at[dy, rows_of(q, BLK)], pm.at[n], 7, (at_pair(q)[0], (y + dy) % NY))
+        for copy in (ra_b, lb_b, rb_b, la_b):
+            copy.start()
+
+    def forward_second():
+        ra_b0.wait_recv()
+        ra_b.wait_recv()
+        fa_b.start()
+        lb_b0.wait_recv()
+        lb_b.wait_recv()
+        fb_b.start()
+
+    early = z < EARLY_PLANES
+
+    @pl.when(early)
+    def _():
+        finish_first()
+
 
     settle(gz.at[pl.ds(0, NZ - 1)], st_recv.at[1])
     total = gz[0]
@@ -350,32 +405,17 @@
     loop(0, width // BLK, lambda k: chol_step(k, work, upper))
     outs.append(pltpu.make_async_copy(upper, upper_out, out_sem.at[len(outs)]))
     outs[-1].start()
-    rb.wait_recv()
-    add_main(left)
-    la.wait_recv()
-    add_main(right)
-    @pl.when(space == 0)
-    def _():
-        m_loc[0] += jnp.dot(tv[0, :, 0:width], upper[...], precision=HIGHEST,
-                            preferred_element_type=F32)
-
-    for swap in swaps:
-        swap.wait_recv()
-    others_t = jnp.concatenate([tb[right], tb[far], tb[left]], axis=0)
-    swapped = products(others_t, gat[y, :, main:part])
-    for r in range(1, NY):
-        m_loc[r] = swapped[(r - 1) * rows:r * rows, :]
-    fa.wait_recv()
-    fb.wait_recv()
-    add_main(far)
-
-    for n, (dx, dc, dy) in enumerate(plane_order):
-        q = pair_at(dx, dc)
-        send(m_loc.at[dy, rows_of(q, BLK)], pm.at[n], 7, (at_pair(q)[0], (y + dy) % NY))
-    ra_b = share(fill, half - fill, cols_b, 11, right)
-    lb_b = share(half + fill, half - fill, cols_b, 12, left)
-    rb_b = share(half, half, cols_b, 13, right)
-    la_b = share(0, half, cols_b, 14, left)
+
+    @pl.when(early)
+    def _():
+        forward_second()
+
+    @pl.when(jnp.logical_not(early))
+    def _():
+        finish_first()
+
+    for block in (left, right, far):
+        put_out(block, cols_a)
     settle(p1f.at[others], st_recv.at[6])
     work[...] = gf[...] + jnp.dot(p1f[...], upper[...], precision=HIGHEST, preferred_element_type=F32)
     work_t[...] = work[...].T
@@ -386,14 +426,22 @@
     for d in range(PLANE - 1):
         total = total + pm[d]
     mz[z] = total
+
+    @pl.when((z == 0) & (pair > 0))
+    def _():
+        settle(t1, st_recv.at[11])
+
+    @pl.when(z == 0)
+    def _():
+        mz[0] += jnp.dot(t1[...], upper[...], precision=HIGHEST, preferred_element_type=F32)
+
     to_z(mz.at[z], 8)
     loop(MIDDLE, width // BLK, lambda k: inverse_step(k, work, work_t))
-    ra_b0.wait_recv()
-    ra_b.wait_recv()
-    fa_b = forward(left, first, cols_b, 15, right)
-    lb_b0.wait_recv()
-    lb_b.wait_recv()
-    fb_b = forward(right, second, cols_b, 16, left)
+
+    @pl.when(jnp.logical_not(early))
+    def _():
+        forward_second()
+
     settle(mz.at[pl.ds(0, NZ - 1)], st_recv.at[8])
     total = mz[0]
     for q in range(1, NZ):
@@ -415,6 +463,11 @@
     for copy in outs:
         copy.wait()
     settle(pr, st_send.at[0])
+
+    @pl.when(space == 0)
+    def _():
+        settle(pm.at[pl.ds(0, PAIRS - 1)], st_send.at[11])
+
     settle(gz.at[pl.ds(0, NZ - 1)], st_send.at[1])
     settle(gf.at[others], st_send.at[2])
 
@@ -499,6 +552,7 @@
             buf(width, width),
             buf(PIECE, width),
             buf(width, width),
+            buf(BLK, width),
             buf(width, width),
             buf(NY, rows, width),
             buf(PLANE - 1, BLK, width),
@@ -510,8 +564,8 @@
             pltpu.SemaphoreType.DMA((17,)),
             pltpu.SemaphoreType.DMA((1 + NY,)),
             pltpu.SemaphoreType.DMA((2 * NY,)),
-            pltpu.SemaphoreType.DMA((11,)),
-            pltpu.SemaphoreType.DMA((11,)),
+            pltpu.SemaphoreType.DMA((12,)),
+            pltpu.SemaphoreType.DMA((12,)),
             pltpu.SemaphoreType.DMA((NY - 1,)),
             pltpu.SemaphoreType.REGULAR((5,)),
         ],

time: 69.9 us -> 66.8 us (0.956)
  Pallas kernels: 69.1 us -> 66.1 us
    pallas_call x1, Pallas kernels: 67.3 us -> 64.3 us  [per_device(): pl.pallas_call(main_kernel, out_shape=(jax.ShapeDtypeStruct((NY, width, p...]
where the time goes in v9:
time: 66.8 us; the launch traced here: 66.7 us
  Pallas kernels  66.1 us (99%)
    pallas_call x1, Pallas kernels, per_device(): pl.pallas_call(main_kernel, out_shape=(jax.ShapeDtypeStruct((NY, width, p...  64.3 us
    pallas_call x1, Pallas kernels, per_device(): pl.pallas_call(functools.partial(update_kernel, -1.0 / math.sqrt(rows_tot...  1.82 us

profile of v9, /device:TPU:1, one launch (start us, length us, event | category | flops | bytes accessed | tf_op | source)
XLA Modules:
  0.0 66.7 jit_solution(12377340759955383803)
XLA Ops:
  0.6 0.0 copy-start
  0.6 64.3 %reduce_factor.1 = (f32[4,128,1920]{2,1,0:T(8,128)S(1)}, f32[128,128]{1,0:T(8,128)S(1)}, f32[64,128]{1,0:T(8,128)S(1)}) custom-call(f32[128,1920]{1,0:T(8,128)} %p_hbm.1, f32[64,7680]{1,0:T(8,128)} %t_ref.1), custom_call_target="tpu_custom_call" | custom-call | tf_op jit(solution)/shard_map/reduce_factor/pallas_call | solution.py:534
  64.9 0.0 copy-done
  64.9 1.8 %apply_update.1 = (f32[128,128]{1,0:T(8,128)}, f32[64,7680]{1,0:T(8,128)}) custom-call(f32[4,128,1920]{2,1,0:T(8,128)S(1)} %get-tuple-element.5.p_ref, f32[64,7680]{1,0:T(8,128)S(1)} %copy-done, f32[64,128]{1,0:T(8,128)S(1)} %get-tuple-element.6.zt_ref, f32[128,128]{1,0:T(8,128)S(1)} %get-tuple-element.7.upper_ref), custom_call_target="tpu_custom_call" | custom-call | tf_op jit(solution)/shard_map/apply_update/pallas_call | solution.py:578
Async XLA Ops:
  0.6 64.3 %copy-start = (f32[64,7680]{1,0:T(8,128)S(1)}, f32[64,7680]{1,0:T(8,128)}, u32[]{:S(2)}) copy-start(f32[64,7680]{1,0:T(8,128)} %t_ref.1) | copy-start | bytes 5898244

commit v10 on v9

--- a/solution.py
+++ b/solution.py
@@ -18,7 +18,7 @@
 LANES = 128
 PIECE = 16
 MIDDLE = 8
-EARLY_PLANES = 7
+EARLY_PLANES = 3
 PLANE = PAIRS * NY
 
 
@@ -234,8 +234,6 @@
     cols_a, cols_b = pl.ds(0, main), pl.ds(main, tail)
     ra = share(0, half, cols_a, 0, right)
     lb = share(half, half, cols_a, 1, left)
-    rb = share(half, half, cols_a, 2, right)
-    la = share(0, half, cols_a, 3, left)
     own.wait()
     high, low = split2(gat[y])
     both = dot_nt(high, jnp.concatenate([high, low], axis=0))
@@ -261,6 +259,8 @@
         total = total + pr[d]
     yr[y] = total
     loop(1, NY, lambda d: send(yr.at[y], yr.at[y], 10, at_y((y + d) % NY)))
+    rb = share(half, half, cols_a, 2, right)
+    la = share(0, half, cols_a, 3, left)
     swaps = []
     for index, target in ((8, right), (9, left), (10, far)):
         cols = pl.ds(pl.multiple_of(target * part + main, LANES), tail)
@@ -333,6 +333,10 @@
     fill = 24
     ra_b0 = share(0, fill, cols_b, 6, right)
     lb_b0 = share(half, fill, cols_b, 7, left)
+    rb.wait_recv()
+    add_main(left)
+    la.wait_recv()
+    add_main(right)
 
     def second(start, size, index, target):
         lines = pl.ds(start, size)
@@ -350,10 +354,6 @@
     fb_b = relay(right, bottom, 16, left)
 
     def finish_first():
-        rb.wait_recv()
-        add_main(left)
-        la.wait_recv()
-        add_main(right)
         for swap in swaps:
             swap.wait_recv()
         others_t = jnp.concatenate([tb[right], tb[far], tb[left]], axis=0)
@@ -377,6 +377,15 @@
         lb_b.wait_recv()
         fb_b.start()
 
+    def reduce_plane():
+        settle(pm, st_recv.at[7])
+        total = m_loc[0, tile, :]
+        for d in range(PLANE - 1):
+            total = total + pm[d]
+        mz[z] = total
+        to_z(mz.at[z], 8)
+
+    tile = rows_of(pair, BLK)
     early = z < EARLY_PLANES
 
     @pl.when(early)
@@ -399,6 +408,18 @@
     p1f[mine, :] = p1s[...]
     to_pairs(lambda q: p1f.at[mine], lambda n: p1f.at[mine], 6)
 
+    @pl.when((z == 0) & (pair > 0))
+    def _():
+        settle(t1, st_recv.at[11])
+
+    @pl.when(z == 0)
+    def _():
+        to_z(t1, 12)
+
+    @pl.when(early)
+    def _():
+        reduce_plane()
+
     others = pl.ds(0, (PAIRS - 1) * PIECE)
     settle(gf.at[others], st_recv.at[2])
     work[...] = gf[...]
@@ -420,30 +441,24 @@
     work[...] = gf[...] + jnp.dot(p1f[...], upper[...], precision=HIGHEST, preferred_element_type=F32)
     work_t[...] = work[...].T
     loop(0, MIDDLE, lambda k: inverse_step(k, work, work_t))
-    settle(pm, st_recv.at[7])
-    tile = rows_of(pair, BLK)
-    total = m_loc[0, tile, :]
-    for d in range(PLANE - 1):
-        total = total + pm[d]
-    mz[z] = total
-
-    @pl.when((z == 0) & (pair > 0))
-    def _():
-        settle(t1, st_recv.at[11])
-
-    @pl.when(z == 0)
-    def _():
-        mz[0] += jnp.dot(t1[...], upper[...], precision=HIGHEST, preferred_element_type=F32)
-
-    to_z(mz.at[z], 8)
+
+    @pl.when(jnp.logical_not(early))
+    def _():
+        reduce_plane()
+
     loop(MIDDLE, width // BLK, lambda k: inverse_step(k, work, work_t))
 
     @pl.when(jnp.logical_not(early))
     def _():
         forward_second()
 
+    @pl.when(z > 0)
+    def _():
+        settle(t1, st_recv.at[12])
+
+    total = jnp.dot(t1[...], upper[...], precision=HIGHEST, preferred_element_type=F32)
     settle(mz.at[pl.ds(0, NZ - 1)], st_recv.at[8])
-    total = mz[0]
+    total = total + mz[0]
     for q in range(1, NZ):
         total = total + mz[q]
     zsum[tile, :] = jnp.dot(total, work[...], precision=HIGHEST, preferred_element_type=F32)
@@ -467,6 +482,10 @@
     @pl.when(space == 0)
     def _():
         settle(pm.at[pl.ds(0, PAIRS - 1)], st_send.at[11])
+
+    @pl.when(z == 0)
+    def _():
+        settle(mz.at[pl.ds(0, NZ - 1)], st_send.at[12])
 
     settle(gz.at[pl.ds(0, NZ - 1)], st_send.at[1])
     settle(gf.at[others], st_send.at[2])
@@ -522,7 +541,7 @@
 def per_device(panel, trailing):
     width, part = panel.shape
     rows, block = trailing.shape
-    tail = part // LANES * 11 // 15 * LANES
+    tail = part // LANES * 8 // 15 * LANES
     rows_total = block * lax.axis_size("space")
     vmem = pl.BlockSpec(memory_space=pltpu.VMEM)
     hbm = pl.BlockSpec(memory_space=pltpu.HBM)
@@ -564,8 +583,8 @@
             pltpu.SemaphoreType.DMA((17,)),
             pltpu.SemaphoreType.DMA((1 + NY,)),
             pltpu.SemaphoreType.DMA((2 * NY,)),
-            pltpu.SemaphoreType.DMA((12,)),
-            pltpu.SemaphoreType.DMA((12,)),
+            pltpu.SemaphoreType.DMA((13,)),
+            pltpu.SemaphoreType.DMA((13,)),
             pltpu.SemaphoreType.DMA((NY - 1,)),
             pltpu.SemaphoreType.REGULAR((5,)),
         ],

time: 66.8 us -> 68.8 us (1.030)
  Pallas kernels: 66.1 us -> 68.1 us
    pallas_call x1, Pallas kernels: 64.3 us -> 66.2 us  [per_device(): pl.pallas_call(main_kernel, out_shape=(jax.ShapeDtypeStruct((NY, width, p...]
where the time goes in v10:
time: 68.8 us; the launch traced here: 68.7 us
  Pallas kernels  68.1 us (99%)
    pallas_call x1, Pallas kernels, per_device(): pl.pallas_call(main_kernel, out_shape=(jax.ShapeDtypeStruct((NY, width, p...  66.2 us
    pallas_call x1, Pallas kernels, per_device(): pl.pallas_call(functools.partial(update_kernel, -1.0 / math.sqrt(rows_tot...  1.81 us

profile of v10, /device:TPU:1, one launch (start us, length us, event | category | flops | bytes accessed | tf_op | source)
XLA Modules:
  0.0 68.7 jit_solution(17063217370801816323)
XLA Ops:
  0.6 0.0 copy-start
  0.6 66.2 %reduce_factor.1 = (f32[4,128,1920]{2,1,0:T(8,128)S(1)}, f32[128,128]{1,0:T(8,128)S(1)}, f32[64,128]{1,0:T(8,128)S(1)}) custom-call(f32[128,1920]{1,0:T(8,128)} %p_hbm.1, f32[64,7680]{1,0:T(8,128)} %t_ref.1), custom_call_target="tpu_custom_call" | custom-call | tf_op jit(solution)/shard_map/reduce_factor/pallas_call | solution.py:553
  66.9 0.0 copy-done
  66.9 1.8 %apply_update.1 = (f32[128,128]{1,0:T(8,128)}, f32[64,7680]{1,0:T(8,128)}) custom-call(f32[4,128,1920]{2,1,0:T(8,128)S(1)} %get-tuple-element.5.p_ref, f32[64,7680]{1,0:T(8,128)S(1)} %copy-done, f32[64,128]{1,0:T(8,128)S(1)} %get-tuple-element.6.zt_ref, f32[128,128]{1,0:T(8,128)S(1)} %get-tuple-element.7.upper_ref), custom_call_target="tpu_custom_call" | custom-call | tf_op jit(solution)/shard_map/apply_update/pallas_call | solution.py:597
Async XLA Ops:
  0.6 66.3 %copy-start = (f32[64,7680]{1,0:T(8,128)S(1)}, f32[64,7680]{1,0:T(8,128)}, u32[]{:S(2)}) copy-start(f32[64,7680]{1,0:T(8,128)} %t_ref.1) | copy-start | bytes 5898244

commit v11 on v8

--- a/solution.py
+++ b/solution.py
@@ -18,6 +18,7 @@
 LANES = 128
 PIECE = 16
 MIDDLE = 8
+EARLY_PLANES = 3
 PLANE = PAIRS * NY
 
 
@@ -229,12 +230,10 @@
         copy.start()
         return copy
 
-    first, second = pl.ds(0, half), pl.ds(half, half)
+    first, second_half = pl.ds(0, half), pl.ds(half, half)
     cols_a, cols_b = pl.ds(0, main), pl.ds(main, tail)
     ra = share(0, half, cols_a, 0, right)
     lb = share(half, half, cols_a, 1, left)
-    rb = share(half, half, cols_a, 2, right)
-    la = share(0, half, cols_a, 3, left)
     own.wait()
     high, low = split2(gat[y])
     both = dot_nt(high, jnp.concatenate([high, low], axis=0))
@@ -260,6 +259,8 @@
         total = total + pr[d]
     yr[y] = total
     loop(1, NY, lambda d: send(yr.at[y], yr.at[y], 10, at_y((y + d) % NY)))
+    rb = share(half, half, cols_a, 2, right)
+    la = share(0, half, cols_a, 3, left)
     swaps = []
     for index, target in ((8, right), (9, left), (10, far)):
         cols = pl.ds(pl.multiple_of(target * part + main, LANES), tail)
@@ -324,10 +325,48 @@
     ra.wait_recv()
     fa = forward(left, first, cols_a, 4, right)
     lb.wait_recv()
-    fb = forward(right, second, cols_a, 5, left)
+    fb = forward(right, second_half, cols_a, 5, left)
     fill = 24
     ra_b0 = share(0, fill, cols_b, 6, right)
     lb_b0 = share(half, fill, cols_b, 7, left)
+
+    def second(start, size, index, target):
+        lines = pl.ds(start, size)
+        return gather_copy(p_hbm.at[lines, cols_b], gat.at[y, lines, cols_b], index, target)
+
+    def relay(block, lines, index, target):
+        ref = gat.at[block, lines, cols_b]
+        return gather_copy(ref, ref, index, target)
+
+    ra_b = second(fill, half - fill, 11, right)
+    lb_b = second(half + fill, half - fill, 12, left)
+    rb_b = second(half, half, 13, right)
+    la_b = second(0, half, 14, left)
+    fa_b = relay(left, first, 15, right)
+    fb_b = relay(right, second_half, 16, left)
+
+    def start_second():
+        for copy in (ra_b, lb_b, rb_b, la_b):
+            copy.start()
+
+    def forward_second():
+        ra_b0.wait_recv()
+        ra_b.wait_recv()
+        fa_b.start()
+        lb_b0.wait_recv()
+        lb_b.wait_recv()
+        fb_b.start()
+
+    early = z < EARLY_PLANES
+
+    @pl.when(early)
+    def _():
+        start_second()
+
+    rb.wait_recv()
+    add_main(left)
+    la.wait_recv()
+    add_main(right)
 
     settle(gz.at[pl.ds(0, NZ - 1)], st_recv.at[1])
     total = gz[0]
@@ -347,13 +386,15 @@
     others = pl.ds(0, (PAIRS - 1) * PIECE)
     settle(gf.at[others], st_recv.at[2])
     work[...] = gf[...]
-    loop(0, width // BLK, lambda k: chol_step(k, work, upper))
+    loop(0, width // BLK // 2, lambda k: chol_step(k, work, upper))
+
+    @pl.when(early)
+    def _():
+        forward_second()
+
+    loop(width // BLK // 2, width // BLK, lambda k: chol_step(k, work, upper))
     outs.append(pltpu.make_async_copy(upper, upper_out, out_sem.at[len(outs)]))
     outs[-1].start()
-    rb.wait_recv()
-    add_main(left)
-    la.wait_recv()
-    add_main(right)
     @pl.when(space == 0)
     def _():
         m_loc[0] += jnp.dot(tv[0, :, 0:width], upper[...], precision=HIGHEST,
@@ -372,10 +413,11 @@
     for n, (dx, dc, dy) in enumerate(plane_order):
         q = pair_at(dx, dc)
         send(m_loc.at[dy, rows_of(q, BLK)], pm.at[n], 7, (at_pair(q)[0], (y + dy) % NY))
-    ra_b = share(fill, half - fill, cols_b, 11, right)
-    lb_b = share(half + fill, half - fill, cols_b, 12, left)
-    rb_b = share(half, half, cols_b, 13, right)
-    la_b = share(0, half, cols_b, 14, left)
+
+    @pl.when(jnp.logical_not(early))
+    def _():
+        start_second()
+
     settle(p1f.at[others], st_recv.at[6])
     work[...] = gf[...] + jnp.dot(p1f[...], upper[...], precision=HIGHEST, preferred_element_type=F32)
     work_t[...] = work[...].T
@@ -388,12 +430,11 @@
     mz[z] = total
     to_z(mz.at[z], 8)
     loop(MIDDLE, width // BLK, lambda k: inverse_step(k, work, work_t))
-    ra_b0.wait_recv()
-    ra_b.wait_recv()
-    fa_b = forward(left, first, cols_b, 15, right)
-    lb_b0.wait_recv()
-    lb_b.wait_recv()
-    fb_b = forward(right, second, cols_b, 16, left)
+
+    @pl.when(jnp.logical_not(early))
+    def _():
+        forward_second()
+
     settle(mz.at[pl.ds(0, NZ - 1)], st_recv.at[8])
     total = mz[0]
     for q in range(1, NZ):
@@ -469,7 +510,7 @@
 def per_device(panel, trailing):
     width, part = panel.shape
     rows, block = trailing.shape
-    tail = part // LANES * 11 // 15 * LANES
+    tail = part // LANES * 7 // 15 * LANES
     rows_total = block * lax.axis_size("space")
     vmem = pl.BlockSpec(memory_space=pltpu.VMEM)
     hbm = pl.BlockSpec(memory_space=pltpu.HBM)

time: 69.9 us -> 69.9 us (level)
  no operation moved by 1% of the time
where the time goes in v11:
time: 69.9 us; the launch traced here: 69.8 us
  Pallas kernels  69.2 us (99%)
    pallas_call x1, Pallas kernels, per_device(): pl.pallas_call(main_kernel, out_shape=(jax.ShapeDtypeStruct((NY, width, p...  67.4 us
    pallas_call x1, Pallas kernels, per_device(): pl.pallas_call(functools.partial(update_kernel, -1.0 / math.sqrt(rows_tot...  1.82 us

profile of v11, /device:TPU:1, one launch (start us, length us, event | category | flops | bytes accessed | tf_op | source)
XLA Modules:
  0.0 69.8 jit_solution(16428342411180120690)
XLA Ops:
  0.6 0.0 copy-start
  0.6 67.4 %reduce_factor.1 = (f32[4,128,1920]{2,1,0:T(8,128)S(1)}, f32[128,128]{1,0:T(8,128)S(1)}, f32[64,128]{1,0:T(8,128)S(1)}) custom-call(f32[128,1920]{1,0:T(8,128)} %p_hbm.1, f32[64,7680]{1,0:T(8,128)} %t_ref.1), custom_call_target="tpu_custom_call" | custom-call | tf_op jit(solution)/shard_map/reduce_factor/pallas_call | solution.py:522
  68.0 0.0 copy-done
  68.0 1.8 %apply_update.1 = (f32[128,128]{1,0:T(8,128)}, f32[64,7680]{1,0:T(8,128)}) custom-call(f32[4,128,1920]{2,1,0:T(8,128)S(1)} %get-tuple-element.5.p_ref, f32[64,7680]{1,0:T(8,128)S(1)} %copy-done, f32[64,128]{1,0:T(8,128)S(1)} %get-tuple-element.6.zt_ref, f32[128,128]{1,0:T(8,128)S(1)} %get-tuple-element.7.upper_ref), custom_call_target="tpu_custom_call" | custom-call | tf_op jit(solution)/shard_map/apply_update/pallas_call | solution.py:565
Async XLA Ops:
  0.6 67.4 %copy-start = (f32[64,7680]{1,0:T(8,128)S(1)}, f32[64,7680]{1,0:T(8,128)}, u32[]{:S(2)}) copy-start(f32[64,7680]{1,0:T(8,128)} %t_ref.1) | copy-start | bytes 5898244

commit v12 on v11

--- a/solution.py
+++ b/solution.py
@@ -386,13 +386,7 @@
     others = pl.ds(0, (PAIRS - 1) * PIECE)
     settle(gf.at[others], st_recv.at[2])
     work[...] = gf[...]
-    loop(0, width // BLK // 2, lambda k: chol_step(k, work, upper))
-
-    @pl.when(early)
-    def _():
-        forward_second()
-
-    loop(width // BLK // 2, width // BLK, lambda k: chol_step(k, work, upper))
+    loop(0, width // BLK, lambda k: chol_step(k, work, upper))
     outs.append(pltpu.make_async_copy(upper, upper_out, out_sem.at[len(outs)]))
     outs[-1].start()
     @pl.when(space == 0)
@@ -413,6 +407,10 @@
     for n, (dx, dc, dy) in enumerate(plane_order):
         q = pair_at(dx, dc)
         send(m_loc.at[dy, rows_of(q, BLK)], pm.at[n], 7, (at_pair(q)[0], (y + dy) % NY))
+
+    @pl.when(early)
+    def _():
+        forward_second()
 
     @pl.when(jnp.logical_not(early))
     def _():

time: 69.9 us -> 65.5 us (0.937)
  Pallas kernels: 69.2 us -> 64.8 us
    pallas_call x1, Pallas kernels: 67.4 us -> 62.9 us  [per_device(): pl.pallas_call(main_kernel, out_shape=(jax.ShapeDtypeStruct((NY, width, p...]
where the time goes in v12:
time: 65.5 us; the launch traced here: 65.4 us
  Pallas kernels  64.8 us (99%)
    pallas_call x1, Pallas kernels, per_device(): pl.pallas_call(main_kernel, out_shape=(jax.ShapeDtypeStruct((NY, width, p...  62.9 us
    pallas_call x1, Pallas kernels, per_device(): pl.pallas_call(functools.partial(update_kernel, -1.0 / math.sqrt(rows_tot...  1.82 us

profile of v12, /device:TPU:1, one launch (start us, length us, event | category | flops | bytes accessed | tf_op | source)
XLA Modules:
  0.0 65.4 jit_solution(1668053664176887351)
XLA Ops:
  0.6 0.0 copy-start
  0.6 62.9 %reduce_factor.1 = (f32[4,128,1920]{2,1,0:T(8,128)S(1)}, f32[128,128]{1,0:T(8,128)S(1)}, f32[64,128]{1,0:T(8,128)S(1)}) custom-call(f32[128,1920]{1,0:T(8,128)} %p_hbm.1, f32[64,7680]{1,0:T(8,128)} %t_ref.1), custom_call_target="tpu_custom_call" | custom-call | tf_op jit(solution)/shard_map/reduce_factor/pallas_call | solution.py:520
  63.6 0.0 copy-done
  63.6 1.8 %apply_update.1 = (f32[128,128]{1,0:T(8,128)}, f32[64,7680]{1,0:T(8,128)}) custom-call(f32[4,128,1920]{2,1,0:T(8,128)S(1)} %get-tuple-element.5.p_ref, f32[64,7680]{1,0:T(8,128)S(1)} %copy-done, f32[64,128]{1,0:T(8,128)S(1)} %get-tuple-element.6.zt_ref, f32[128,128]{1,0:T(8,128)S(1)} %get-tuple-element.7.upper_ref), custom_call_target="tpu_custom_call" | custom-call | tf_op jit(solution)/shard_map/apply_update/pallas_call | solution.py:563
Async XLA Ops:
  0.6 63.0 %copy-start = (f32[64,7680]{1,0:T(8,128)S(1)}, f32[64,7680]{1,0:T(8,128)}, u32[]{:S(2)}) copy-start(f32[64,7680]{1,0:T(8,128)} %t_ref.1) | copy-start | bytes 5898244

commit v13 on v8

--- a/solution.py
+++ b/solution.py
@@ -17,7 +17,7 @@
 BLK = 8
 LANES = 128
 PIECE = 16
-MIDDLE = 8
+EARLY, MIDDLE = 5, 12
 PLANE = PAIRS * NY
 
 
@@ -233,8 +233,6 @@
     cols_a, cols_b = pl.ds(0, main), pl.ds(main, tail)
     ra = share(0, half, cols_a, 0, right)
     lb = share(half, half, cols_a, 1, left)
-    rb = share(half, half, cols_a, 2, right)
-    la = share(0, half, cols_a, 3, left)
     own.wait()
     high, low = split2(gat[y])
     both = dot_nt(high, jnp.concatenate([high, low], axis=0))
@@ -260,6 +258,8 @@
         total = total + pr[d]
     yr[y] = total
     loop(1, NY, lambda d: send(yr.at[y], yr.at[y], 10, at_y((y + d) % NY)))
+    rb = share(half, half, cols_a, 2, right)
+    la = share(0, half, cols_a, 3, left)
     swaps = []
     for index, target in ((8, right), (9, left), (10, far)):
         cols = pl.ds(pl.multiple_of(target * part + main, LANES), tail)
@@ -325,7 +325,7 @@
     fa = forward(left, first, cols_a, 4, right)
     lb.wait_recv()
     fb = forward(right, second, cols_a, 5, left)
-    fill = 24
+    fill = 32
     ra_b0 = share(0, fill, cols_b, 6, right)
     lb_b0 = share(half, fill, cols_b, 7, left)
 
@@ -354,6 +354,11 @@
     add_main(left)
     la.wait_recv()
     add_main(right)
+    settle(p1f.at[others], st_recv.at[6])
+    work[...] = gf[...] + jnp.dot(p1f[...], upper[...], precision=HIGHEST, preferred_element_type=F32)
+    work_t[...] = work[...].T
+    loop(0, EARLY, lambda k: inverse_step(k, work, work_t))
+
     @pl.when(space == 0)
     def _():
         m_loc[0] += jnp.dot(tv[0, :, 0:width], upper[...], precision=HIGHEST,
@@ -376,10 +381,7 @@
     lb_b = share(half + fill, half - fill, cols_b, 12, left)
     rb_b = share(half, half, cols_b, 13, right)
     la_b = share(0, half, cols_b, 14, left)
-    settle(p1f.at[others], st_recv.at[6])
-    work[...] = gf[...] + jnp.dot(p1f[...], upper[...], precision=HIGHEST, preferred_element_type=F32)
-    work_t[...] = work[...].T
-    loop(0, MIDDLE, lambda k: inverse_step(k, work, work_t))
+    loop(EARLY, MIDDLE, lambda k: inverse_step(k, work, work_t))
     settle(pm, st_recv.at[7])
     tile = rows_of(pair, BLK)
     total = m_loc[0, tile, :]
@@ -469,7 +471,7 @@
 def per_device(panel, trailing):
     width, part = panel.shape
     rows, block = trailing.shape
-    tail = part // LANES * 11 // 15 * LANES
+    tail = part // LANES * 2 // 5 * LANES
     rows_total = block * lax.axis_size("space")
     vmem = pl.BlockSpec(memory_space=pltpu.VMEM)
     hbm = pl.BlockSpec(memory_space=pltpu.HBM)

time: 69.9 us -> 65.3 us (0.934)
  Pallas kernels: 69.1 us -> 64.5 us
    pallas_call x1, Pallas kernels: 67.3 us -> 62.7 us  [per_device(): pl.pallas_call(main_kernel, out_shape=(jax.ShapeDtypeStruct((NY, width, p...]
where the time goes in v13:
time: 65.3 us; the launch traced here: 65.2 us
  Pallas kernels  64.5 us (99%)
    pallas_call x1, Pallas kernels, per_device(): pl.pallas_call(main_kernel, out_shape=(jax.ShapeDtypeStruct((NY, width, p...  62.7 us
    pallas_call x1, Pallas kernels, per_device(): pl.pallas_call(functools.partial(update_kernel, -1.0 / math.sqrt(rows_tot...  1.81 us

profile of v13, /device:TPU:1, one launch (start us, length us, event | category | flops | bytes accessed | tf_op | source)
XLA Modules:
  0.0 65.2 jit_solution(6608375121458355909)
XLA Ops:
  0.6 0.0 copy-start
  0.6 62.7 %reduce_factor.1 = (f32[4,128,1920]{2,1,0:T(8,128)S(1)}, f32[128,128]{1,0:T(8,128)S(1)}, f32[64,128]{1,0:T(8,128)S(1)}) custom-call(f32[128,1920]{1,0:T(8,128)} %p_hbm.1, f32[64,7680]{1,0:T(8,128)} %t_ref.1), custom_call_target="tpu_custom_call" | custom-call | tf_op jit(solution)/shard_map/reduce_factor/pallas_call | solution.py:483
  63.4 0.0 copy-done
  63.4 1.8 %apply_update.1 = (f32[128,128]{1,0:T(8,128)}, f32[64,7680]{1,0:T(8,128)}) custom-call(f32[4,128,1920]{2,1,0:T(8,128)S(1)} %get-tuple-element.5.p_ref, f32[64,7680]{1,0:T(8,128)S(1)} %copy-done, f32[64,128]{1,0:T(8,128)S(1)} %get-tuple-element.6.zt_ref, f32[128,128]{1,0:T(8,128)S(1)} %get-tuple-element.7.upper_ref), custom_call_target="tpu_custom_call" | custom-call | tf_op jit(solution)/shard_map/apply_update/pallas_call | solution.py:526
Async XLA Ops:
  0.6 62.7 %copy-start = (f32[64,7680]{1,0:T(8,128)S(1)}, f32[64,7680]{1,0:T(8,128)}, u32[]{:S(2)}) copy-start(f32[64,7680]{1,0:T(8,128)} %t_ref.1) | copy-start | bytes 5898244
